TPU v7x, 32 devices: a whole 2x2x4 slice. The times are simulated.
32 devices in a mesh: dp: 4 (over y, x), seq: 8 (over z, core).
Axes of the slice: x: 2, y: 2, z: 4, core: 2. Of those that a mesh axis runs over, the one named last changes fastest.
Arguments:
- inputs: bfloat16 [8, 2048, 512], P('dp', 'seq'), may hold values from -6 to 6
- w_qkv: bfloat16 [512, 1536], P(('dp', 'seq')), may hold values from -0.25 to 0.25
- bias_qv: bfloat16 [2, 512], P(None, ('dp', 'seq')), may hold values from -1.796875 to 1.796875
- w_out: bfloat16 [512, 512], P(('dp', 'seq')), may hold values from -1 to 1
- bias_out: bfloat16 [512], P(('dp', 'seq')), may hold values from -1.796875 to 1.796875
- w_in: bfloat16 [512, 2048], P(('dp', 'seq')), may hold values from -0.25 to 0.25
- bias_in: bfloat16 [2048], P(('dp', 'seq')), may hold values from -1.796875 to 1.796875
- w_back: bfloat16 [2048, 512], P(('dp', 'seq')), may hold values from -0.1875 to 0.1875
- bias_back: bfloat16 [512], P(('dp', 'seq')), may hold values from -1.796875 to 1.796875
- alphas: float32 [2], replicated, may hold values from 0.2 to 0.4
- cotangent: bfloat16 [8, 2048, 512], P('dp', 'seq'), may hold values from -6 to 6
Outputs:
- outputs: bfloat16 [8, 2048, 512], P('dp', 'seq')
- grad_inputs: bfloat16 [8, 2048, 512], P('dp', 'seq')
- grad_w_qkv: float32 [512, 1536], P(('dp', 'seq'))
- grad_bias_qv: float32 [2, 512], P(None, ('dp', 'seq'))
- grad_w_out: float32 [512, 512], P(('dp', 'seq'))
- grad_bias_out: float32 [512], P(('dp', 'seq'))
- grad_w_in: float32 [512, 2048], P(('dp', 'seq'))
- grad_bias_in: float32 [2048], P(('dp', 'seq'))
- grad_w_back: float32 [2048, 512], P(('dp', 'seq'))
- grad_bias_back: float32 [512], P(('dp', 'seq'))
- grad_alphas: float32 [2], replicated
All inputs are finite; a program needn't handle non-finite values.
Results may differ from a plain program's by a relative error of at most 0.038.
Values may be sent and summed in bfloat16 or wider, within the bound.
No kernel may reach another device: no remote copies, remote signals or barrier semaphores. Data moves between devices by JAX's collectives and lax.ppermute only.
A program may use at most 128 MiB of HBM per device.

v0:
```python
import math

import jax
import jax.numpy as jnp
from jax import lax
from jax.sharding import PartitionSpec as P

D = 512
HEADS = 8
HEAD_DIM = 64
BLOCK = 256
MB = 2
SEQ_MB = 1


def tdot(left, right):
    return lax.dot_general(
        left, right, (((0,), (0,)), ((), ())), preferred_element_type=jnp.float32
    )


def ndot(left, right):
    return lax.dot_general(
        left, right, (((1,), (1,)), ((), ())), preferred_element_type=jnp.float32
    )


def smooth_gate(values):
    return jax.nn.gelu(values, approximate=True)


def block_split(pieces):
    count = pieces.shape[1]
    width = math.gcd(count, 512)
    number = count // width
    split = pieces.reshape(pieces.shape[0], number, width, pieces.shape[2])
    return (jnp.transpose(split, (1, 0, 2, 3)), width, number)


def body(
    inputs, w_qkv, bias_qv, w_out, bias_out, w_in, bias_in, w_back, bias_back, alphas, cotangent
):
    group = inputs.shape[1]
    rows = SEQ_MB * group
    scale = 1.0 / math.sqrt(HEAD_DIM)
    q_start = lax.axis_index("seq") * group
    query_block = (q_start + jnp.arange(group, dtype=jnp.int32)) // BLOCK
    alpha_attn = alphas[0]
    alpha_ffn = alphas[1]
    params = (w_qkv, w_out, w_in, w_back, bias_qv, bias_out, bias_in, bias_back)
    out_list = []
    grad_list = []
    accum_grads = None
    attn_alpha_grad = jnp.zeros((), jnp.float32)
    ffn_alpha_grad = jnp.zeros((), jnp.float32)
    for micro in range(MB):
        forward_params = (
            lax.all_gather(params[0], ("dp", "seq"), axis=0, tiled=True),
            lax.all_gather(params[1], ("dp", "seq"), axis=0, tiled=True),
            lax.all_gather(params[2], ("dp", "seq"), axis=0, tiled=True),
            lax.all_gather(params[3], ("dp", "seq"), axis=0, tiled=True),
            lax.all_gather(params[4], ("dp", "seq"), axis=1, tiled=True),
            lax.all_gather(params[5], ("dp", "seq"), axis=0, tiled=True),
            lax.all_gather(params[6], ("dp", "seq"), axis=0, tiled=True),
            lax.all_gather(params[7], ("dp", "seq"), axis=0, tiled=True),
        )
        wq, wo, wi, wb, bqv, bo, bi, bb = forward_params
        if accum_grads is None:
            accum_grads = [jnp.zeros(p.shape, jnp.float32) for p in forward_params]
        x_rows = inputs[micro * SEQ_MB : (micro + 1) * SEQ_MB].reshape(rows, D)
        qkv_bias = jnp.concatenate([bqv[0], jnp.zeros_like(bqv[0]), bqv[1]]).astype(jnp.float32)
        qkv = (jnp.dot(x_rows, wq, preferred_element_type=jnp.float32) + qkv_bias).astype(
            jnp.bfloat16
        )
        queries = qkv[:, :D].reshape(SEQ_MB, group, HEADS, HEAD_DIM)
        kv_local = qkv[:, D:].reshape(SEQ_MB, group, 2 * D)
        kv_gathered = lax.all_gather(kv_local, "seq", axis=1, tiled=True)
        f_split, f_width, f_number = block_split(kv_gathered)
        f_starts = jnp.arange(f_number, dtype=jnp.int32) * f_width

        def masked_scores(kv_blk, kstart):
            keys = kv_blk[:, :, :D].reshape(SEQ_MB, f_width, HEADS, HEAD_DIM)
            values = kv_blk[:, :, D:].reshape(SEQ_MB, f_width, HEADS, HEAD_DIM)
            scores = (
                jnp.einsum("sqhd,skhd->shqk", queries, keys, preferred_element_type=jnp.float32)
                * scale
            )
            key_block = (kstart + jnp.arange(f_width, dtype=jnp.int32)) // BLOCK
            allowed = key_block[None, :] <= query_block[:, None]
            return (jnp.where(allowed[None, None], scores, -1e30), allowed, values)

        def stats_update(state, kv_blk, kstart):
            maxima, totals = state
            scores, allowed, unused = masked_scores(kv_blk, kstart)
            new_max = jnp.maximum(maxima, jnp.max(scores, axis=-1))
            weights = jnp.where(allowed[None, None], jnp.exp(scores - new_max[..., None]), 0.0)
            totals = totals * jnp.exp(maxima - new_max) + jnp.sum(weights, axis=-1)
            return (new_max, totals)

        def stats_step(state, item):
            kv_blk, kstart = item
            state = stats_update(state, kv_blk, kstart)
            return (state, None)

        start_stats = (
            jnp.full((SEQ_MB, HEADS, group), -1e30, jnp.float32),
            jnp.zeros((SEQ_MB, HEADS, group), jnp.float32),
        )
        (maxima, totals), unused_stats = lax.scan(stats_step, start_stats, (f_split, f_starts))
        log_total = maxima + jnp.log(totals)

        def value_update(accum, kv_blk, kstart):
            scores, allowed, values = masked_scores(kv_blk, kstart)
            probs = jnp.where(allowed[None, None], jnp.exp(scores - log_total[..., None]), 0.0)
            return accum + jnp.einsum(
                "shqk,skhd->sqhd",
                probs.astype(jnp.bfloat16),
                values,
                preferred_element_type=jnp.float32,
            )

        def value_step(accum, item):
            kv_blk, kstart = item
            accum = value_update(accum, kv_blk, kstart)
            return (accum, None)

        attended, unused_values = lax.scan(
            value_step,
            jnp.zeros((SEQ_MB, group, HEADS, HEAD_DIM), jnp.float32),
            (f_split, f_starts),
        )
        mixed = attended.astype(jnp.bfloat16).reshape(rows, D)
        attn = jnp.dot(mixed, wo, preferred_element_type=jnp.float32) + bo.astype(jnp.float32)
        first = x_rows.astype(jnp.float32) + alpha_attn * attn
        hidden = first.astype(jnp.bfloat16)
        pre = jnp.dot(hidden, wi, preferred_element_type=jnp.float32) + bi.astype(jnp.float32)
        gate_value, gate_pull = jax.vjp(smooth_gate, pre)
        gated = gate_value.astype(jnp.bfloat16)
        branch = jnp.dot(gated, wb, preferred_element_type=jnp.float32) + bb.astype(jnp.float32)
        out_list.append((first + alpha_ffn * branch).astype(jnp.bfloat16))
        backward_params = (
            lax.all_gather(params[0], ("dp", "seq"), axis=0, tiled=True),
            lax.all_gather(params[1], ("dp", "seq"), axis=0, tiled=True),
            lax.all_gather(params[2], ("dp", "seq"), axis=0, tiled=True),
            lax.all_gather(params[3], ("dp", "seq"), axis=0, tiled=True),
            lax.all_gather(params[4], ("dp", "seq"), axis=1, tiled=True),
            lax.all_gather(params[5], ("dp", "seq"), axis=0, tiled=True),
            lax.all_gather(params[6], ("dp", "seq"), axis=0, tiled=True),
            lax.all_gather(params[7], ("dp", "seq"), axis=0, tiled=True),
        )
        wq, wo, wi, wb, bqv, bo, bi, bb = backward_params
        upstream = (
            cotangent[micro * SEQ_MB : (micro + 1) * SEQ_MB].reshape(rows, D).astype(jnp.float32)
        )
        ffn_alpha_grad = ffn_alpha_grad + jnp.sum(upstream * branch)
        d_branch = (alpha_ffn * upstream).astype(jnp.bfloat16)
        d_gated = ndot(d_branch, wb).astype(jnp.bfloat16)
        d_pre = gate_pull(d_gated.astype(jnp.float32))[0].astype(jnp.bfloat16)
        d_first = upstream + ndot(d_pre, wi)
        attn_alpha_grad = attn_alpha_grad + jnp.sum(d_first * attn)
        d_attn = (alpha_attn * d_first).astype(jnp.bfloat16)
        d_mixed = ndot(d_attn, wo).astype(jnp.bfloat16).reshape(SEQ_MB, group, HEADS, HEAD_DIM)
        delta = jnp.transpose(jnp.sum(d_mixed.astype(jnp.float32) * attended, axis=-1), (0, 2, 1))
        kv_whole = lax.all_gather(kv_local, "seq", axis=1, tiled=True)
        split, width, number = block_split(kv_whole)
        starts = jnp.arange(number, dtype=jnp.int32) * width

        def back_update(d_query, kv_blk, kstart):
            keys = kv_blk[:, :, :D].reshape(SEQ_MB, width, HEADS, HEAD_DIM)
            values = kv_blk[:, :, D:].reshape(SEQ_MB, width, HEADS, HEAD_DIM)
            scores = (
                jnp.einsum("sqhd,skhd->shqk", queries, keys, preferred_element_type=jnp.float32)
                * scale
            )
            key_block = (kstart + jnp.arange(width, dtype=jnp.int32)) // BLOCK
            allowed = key_block[None, :] <= query_block[:, None]
            probs = jnp.where(allowed[None, None], jnp.exp(scores - log_total[..., None]), 0.0)
            d_probs = jnp.einsum(
                "sqhd,skhd->shqk", d_mixed, values, preferred_element_type=jnp.float32
            )
            d_scores = (probs * (d_probs - delta[..., None])).astype(jnp.bfloat16)
            d_query = (
                d_query
                + jnp.einsum("shqk,skhd->sqhd", d_scores, keys, preferred_element_type=jnp.float32)
                * scale
            )
            d_keys = (
                jnp.einsum("shqk,sqhd->skhd", d_scores, queries, preferred_element_type=jnp.float32)
                * scale
            )
            d_values = jnp.einsum(
                "shqk,sqhd->skhd",
                probs.astype(jnp.bfloat16),
                d_mixed,
                preferred_element_type=jnp.float32,
            )
            both = jnp.concatenate(
                [d_keys.reshape(SEQ_MB, width, D), d_values.reshape(SEQ_MB, width, D)], axis=-1
            )
            return (d_query, both)

        def back_step(d_query, item):
            kv_blk, kstart = item
            return back_update(d_query, kv_blk, kstart)

        d_query, kv_terms = lax.scan(
            back_step, jnp.zeros((SEQ_MB, group, HEADS, HEAD_DIM), jnp.float32), (split, starts)
        )
        kv_terms = jnp.transpose(kv_terms, (1, 0, 2, 3)).reshape(SEQ_MB, number * width, 2 * D)
        kv_mine = lax.psum_scatter(
            kv_terms.astype(jnp.bfloat16), "seq", scatter_dimension=1, tiled=True
        ).astype(jnp.float32)
        d_qkv = jnp.concatenate(
            [d_query.reshape(rows, D), kv_mine.reshape(rows, 2 * D)], axis=-1
        ).astype(jnp.bfloat16)
        d_qkv_wide = d_qkv.astype(jnp.float32)
        grad_list.append((d_first + ndot(d_qkv, wq)).astype(jnp.bfloat16))
        bias_terms = jnp.stack(
            [jnp.sum(d_qkv_wide[:, :D], axis=0), jnp.sum(d_qkv_wide[:, 2 * D :], axis=0)]
        )
        updates = [
            tdot(x_rows, d_qkv),
            tdot(mixed, d_attn),
            tdot(hidden, d_pre),
            tdot(gated, d_branch),
            bias_terms,
            jnp.sum(d_attn.astype(jnp.float32), axis=0),
            jnp.sum(d_pre.astype(jnp.float32), axis=0),
            jnp.sum(d_branch.astype(jnp.float32), axis=0),
        ]
        accum_grads = [a + u for a, u in zip(accum_grads, updates)]
    owned = (
        lax.psum_scatter(accum_grads[0], ("dp", "seq"), scatter_dimension=0, tiled=True),
        lax.psum_scatter(accum_grads[1], ("dp", "seq"), scatter_dimension=0, tiled=True),
        lax.psum_scatter(accum_grads[2], ("dp", "seq"), scatter_dimension=0, tiled=True),
        lax.psum_scatter(accum_grads[3], ("dp", "seq"), scatter_dimension=0, tiled=True),
        lax.psum_scatter(accum_grads[4], ("dp", "seq"), scatter_dimension=1, tiled=True),
        lax.psum_scatter(accum_grads[5], ("dp", "seq"), scatter_dimension=0, tiled=True),
        lax.psum_scatter(accum_grads[6], ("dp", "seq"), scatter_dimension=0, tiled=True),
        lax.psum_scatter(accum_grads[7], ("dp", "seq"), scatter_dimension=0, tiled=True),
    )
    alpha_total = lax.psum(jnp.stack([attn_alpha_grad, ffn_alpha_grad]), ("dp", "seq"))
    outputs = jnp.concatenate(out_list, axis=0).reshape(MB * SEQ_MB, group, D)
    grad_inputs = jnp.concatenate(grad_list, axis=0).reshape(MB * SEQ_MB, group, D)
    return (
        outputs,
        grad_inputs,
        owned[0],
        owned[4],
        owned[1],
        owned[5],
        owned[2],
        owned[6],
        owned[3],
        owned[7],
        alpha_total,
    )


def solution(mesh):
    return jax.shard_map(
        body,
        mesh=mesh,
        in_specs=(
            P("dp", "seq", None),
            P(("dp", "seq"), None),
            P(None, ("dp", "seq")),
            P(("dp", "seq"), None),
            P(("dp", "seq")),
            P(("dp", "seq"), None),
            P(("dp", "seq")),
            P(("dp", "seq"), None),
            P(("dp", "seq")),
            P(),
            P("dp", "seq", None),
        ),
        out_specs=(
            P("dp", "seq", None),
            P("dp", "seq", None),
            P(("dp", "seq"), None),
            P(None, ("dp", "seq")),
            P(("dp", "seq"), None),
            P(("dp", "seq")),
            P(("dp", "seq"), None),
            P(("dp", "seq")),
            P(("dp", "seq"), None),
            P(("dp", "seq")),
            P(),
        ),
        check_vma=False,
    )
```

profile of v0, /device:TPU:0, one launch (start us, length us, event | category | flops | bytes accessed | tf_op | source)
XLA Modules:
  0.0 1109.2 jit_solution(15573458283594505335)
XLA Ops:
  8.0 43.2 %all-gather.2 = bf16[32,16,2]{1,2,0:T(2,128)(2,1)S(1)} all-gather(bf16[1,16,2]{1,2,0:T(2,128)(2,1)} %bitcast.553), channel_id=1, replica_groups=mesh['dp'=4,'seq'=8] {'dp','seq'}, dimensions={0}, use_global_device_ids=true | all-gather | bytes 2112 | tf_op jit(solution)/shard_map/all_gather | solution.py:62
  51.4 17.5 %all-gather.9.cloned.1.call-done = bf16[512,1536]{1,0:T(8,128)(2,1)} async-done(((bf16[16,1536]{1,0:T(8,128)(2,1)}), bf16[512,1536]{1,0:T(8,128)(2,1)}) %all-gather.9.cloned.1.call-update) | async-done | bytes 1572880 | tf_op jit(solution)/shard_map/all_gather | solution.py:58
  78.0 41.7 %all-reduce.7 = (bf16[512]{0:T(512)(128)(2,1)S(1)}, bf16[512]{0:T(512)(128)(2,1)S(1)}, bf16[2048]{0:T(1024)(128)(2,1)S(1)}) all-reduce(bf16[512]{0:T(512)(128)(2,1)S(1)} %dynamic-update-slice.2, bf16[512]{0:T(512)(128)(2,1)S(1)} %dynamic-update-slice, bf16[2048]{0:T(1024)(128)(2,1)S(1)} %dynamic-update-slice.1), channel_id=1, replica_groups=mesh['dp'=4,'seq'=8] {'dp','seq'}, use_global_device_ids=true, to_apply=%add.2 | all-reduce | flops 3072 | bytes 12288
  121.5 45.3 %all_gather.23 = bf16[512,512]{1,0:T(8,128)(2,1)S(1)} all-gather(bf16[16,512]{1,0:T(8,128)(2,1)S(1)} %copy-done.57), channel_id=1, replica_groups=mesh['dp'=4,'seq'=8] {'dp','seq'}, dimensions={0}, use_global_device_ids=true | all-gather | bytes 540672 | tf_op jit(solution)/shard_map/all_gather | solution.py:59
  168.3 6.2 copy.107
  174.5 21.3 %while.88 = (s32[]{:T(128)}, f32[1,8,256]{2,1,0:T(8,128)S(1)}, f32[1,8,256]{2,1,0:T(8,128)S(1)}, s32[4]{0:T(128)}, bf16[4,1,512,1024]{2,3,1,0:T(8,128)(2,1)}, /*...) while((s32[]{:T(128)}, f32[1,8,256]{2,1,0:T(8,128)S(1)}, ...), condition=%wide.region_9.10_spmd.clone, body=%wide.region_6.9_spmd.clone.sunk | while | flops 142759936 | bytes 12826760 | solution.py:109
  195.9 26.4 %while.89 = (s32[]{:T(128)}, f32[1,256,8,64]{1,3,2,0:T(8,128)}, bf16[4,1,512,1024]{2,3,1,0:T(8,128)(2,1)}, s32[4]{0:T(128)}, bf16[1,256,8,64]{1,3,2,0:T(8,128)(2...) while((s32[]{:T(128)}, f32[1,256,8,64]{1,3,2,0:T(8,128)}, ...), condition=%wide.region_11.12_spmd.clone, body=%wide.region_10.11_spmd.clone.sunk | while | flops 274083840 | bytes 6830215 | solution.py:127
  205.2 3.4 fusion.257
  212.0 3.4 fusion.257
  218.9 3.4 fusion.257
  224.0 6.3 copy.104
  230.3 21.3 %while.86 = (s32[]{:T(128)}, f32[1,8,256]{2,1,0:T(8,128)S(1)}, f32[1,8,256]{2,1,0:T(8,128)S(1)}, s32[4]{0:T(128)}, bf16[4,1,512,1024]{2,3,1,0:T(8,128)(2,1)}, /*...) while((s32[]{:T(128)}, f32[1,8,256]{2,1,0:T(8,128)S(1)}, ...), condition=%wide.region_3.4_spmd.clone, body=%wide.region_0.3_spmd.clone.sunk | while | flops 142759936 | bytes 12826760 | solution.py:109
  252.3 23.5 %while.87 = (s32[]{:T(128)}, f32[1,256,8,64]{1,3,2,0:T(8,128)S(1)}, bf16[4,1,512,1024]{2,3,1,0:T(8,128)(2,1)}, s32[4]{0:T(128)}, bf16[1,256,8,64]{1,3,2,0:T(8,12...) while((s32[]{:T(128)}, f32[1,256,8,64]{1,3,2,0:T(8,128)S(1)}, ...), condition=%wide.region_5.6_spmd.clone, body=%wide.region_4.5_spmd.clone.sunk | while | flops 274083840 | bytes 6830215 | solution.py:127
  279.1 3.8 convolution_add_fusion.6
  284.9 2.5 all-gather.13.cloned.1.call-done
  287.4 3.2 convolution_add_fusion.11
  295.1 2.5 convert_reduce_fusion
  299.4 4.0 multiply_reduce_fusion
  305.3 2.5 broadcast.781.clone2
  307.8 38.7 %while.91 = (s32[]{:T(128)}, f32[1,256,8,64]{1,3,2,0:T(8,128)S(1)}, bf16[4,1,512,1024]{3,2,0,1:T(8,128)(2,1)}, bf16[4,1,512,1024]{2,3,1,0:T(8,128)(2,1)}, s32[4]...) while((s32[]{:T(128)}, f32[1,256,8,64]{1,3,2,0:T(8,128)S(1)}, ...), condition=%wide.region_18.19_spmd.clone, body=%wide.region_17.18_spmd.clone.sunk | while | flops 684732416 | bytes 36600024 | solution.py:206
  346.6 2.5 broadcast.781.clone2.1
  349.2 44.2 %while.90 = (s32[]{:T(128)}, f32[1,256,8,64]{1,3,2,0:T(8,128)S(1)}, bf16[4,1,512,1024]{3,2,0,1:T(8,128)(2,1)}, bf16[4,1,512,1024]{2,3,1,0:T(8,128)(2,1)}, s32[4]...) while((s32[]{:T(128)}, f32[1,256,8,64]{1,3,2,0:T(8,128)S(1)}, ...), condition=%wide.region_14.15_spmd.clone, body=%wide.region_13.14_spmd.clone.sunk | while | flops 684732416 | bytes 36600024 | solution.py:206
  396.9 49.2 %reduce-scatter.12.cloned.1.call-done = bf16[1,256,1024]{2,1,0:T(8,128)(2,1)} async-done(((bf16[1,2048,1024]{2,1,0:T(8,128)(2,1)}), bf16[1,256,1024]{2,1,0:T(8,128)(2,1)}) %reduce-scatter.12.cloned.1.call-update) | async-done | bytes 524304 | tf_op jit(solution)/shard_map/reduce_scatter | solution.py:210
  451.0 2.7 fusion.138
  453.8 3.9 convolution_add_fusion.1
  459.7 2.8 convolution_add_fusion.2
  470.8 38.0 %all-reduce.6 = (f32[512]{0:T(512)S(1)}, f32[2048]{0:T(1024)S(1)}, f32[512]{0:T(512)S(1)}, f32[2]{0:T(128)}) all-reduce(f32[512]{0:T(512)S(1)} %add.392, f32[2048]{0:T(1024)S(1)} %add.394, f32[512]{0:T(512)S(1)} %add.396, f32[2]{0:T(128)S(1)} %pad_maximum_fusion.8), channel_id=9, replica_groups=mesh['dp'=4,'seq'=8] {'dp','seq'}, use_global_device_ids=true, to_apply=%region_29.30.clone | all-reduce | flops 3074 | bytes 24592
  515.0 65.2 %reduce-scatter.24.cloned.1.call-done = f32[16,2]{1,0:T(8,128)} async-done(((f32[512,2]{1,0:T(8,128)}), f32[16,2]{1,0:T(8,128)}) %reduce-scatter.24.cloned.1.call-update) | async-done | bytes 144
  581.5 132.7 %reduce-scatter.16.cloned.1.call-done = f32[16,512]{1,0:T(8,128)} async-done(((f32[512,512]{1,0:T(8,128)}), f32[16,512]{1,0:T(8,128)}) %reduce-scatter.16.cloned.1.call-update) | async-done | bytes 32784 | tf_op jit(solution)/shard_map/reduce_scatter | solution.py:234
  714.3 141.4 %reduce-scatter.20.cloned.1.call-done = f32[64,512]{1,0:T(8,128)} async-done(((f32[2048,512]{1,0:T(8,128)}), f32[64,512]{1,0:T(8,128)}) %reduce-scatter.20.cloned.1.call-update) | async-done | bytes 131088 | tf_op jit(solution)/shard_map/reduce_scatter | solution.py:236
  855.6 142.5 %reduce-scatter.18.cloned.1.call-done = f32[16,2048]{1,0:T(8,128)} async-done(((f32[512,2048]{1,0:T(8,128)}), f32[16,2048]{1,0:T(8,128)}) %reduce-scatter.18.cloned.1.call-update) | async-done | bytes 131088 | tf_op jit(solution)/shard_map/reduce_scatter | solution.py:235
  998.1 104.0 %reduce-scatter.22.cloned.1.call-done = f32[16,1536]{1,0:T(8,128)} async-done(((f32[512,1536]{1,0:T(8,128)}), f32[16,1536]{1,0:T(8,128)}) %reduce-scatter.22.cloned.1.call-update) | async-done | bytes 98320
  (515 shorter events, 215.5 us)
Async XLA Ops:
  7.2 61.7 %all-gather.9.cloned.1.call-start = ((), (), s32[]{:S(2)}) async-start(), calls=%async_computation.7 | async-start | bytes 1622016 | tf_op jit(solution)/shard_map/all_gather | solution.py:58
  7.9 160.4 %all-gather.17.cloned.1.call-start = ((), (), s32[]{:S(2)}) async-start(), calls=%async_computation.16 | async-start | bytes 4718592 | tf_op jit(solution)/shard_map/all_gather | solution.py:77
  51.3 20.6 %copy-start.30 = (bf16[2,256,512]{2,1,0:T(8,128)(2,1)S(1)}, bf16[2,256,512]{2,1,0:T(8,128)(2,1)}, u32[]{:S(2)}) copy-start(bf16[2,256,512]{2,1,0:T(8,128)(2,1)} %param.23) | copy-start | bytes 1572868
  71.9 5.7 copy-start.65
  71.9 5.9 copy-start.66
  71.9 49.6 %copy-start.57 = (bf16[16,512]{1,0:T(8,128)(2,1)S(1)}, bf16[16,512]{1,0:T(8,128)(2,1)}, u32[]{:S(2)}) copy-start(bf16[16,512]{1,0:T(8,128)(2,1)} %param.26) | copy-start | bytes 49156
  71.9 152.1 %all-gather.15.cloned.1.call-start = ((), (), s32[]{:S(2)}) async-start(), calls=%async_computation.15 | async-start | bytes 4718592 | tf_op jit(solution)/shard_map/all_gather | solution.py:77
  73.9 46.9 %copy-start.51 = (bf16[256,1536]{1,0:T(8,128)(2,1)}, bf16[256,1536]{1,0:T(8,128)(2,1)S(1)}, u32[]{:S(2)}) copy-start(bf16[256,1536]{1,0:T(8,128)(2,1)S(1)} %fusion.95) | copy-start | bytes 2359300
  75.0 204.1 %all-gather.11.cloned.1.call-start = ((), (), s32[]{:S(2)}) async-start(), calls=%async_computation.8 | async-start | bytes 2162688 | tf_op jit(solution)/shard_map/all_gather | solution.py:60
  75.5 211.9 %all-gather.13.cloned.1.call-start = ((), (), s32[]{:S(2)}) async-start(), calls=%async_computation.9 | async-start | bytes 2162688 | tf_op jit(solution)/shard_map/all_gather | solution.py:61
  76.1 319.5 %reduce-scatter.14.cloned.1.call-start = ((), (), s32[]{:S(2)}) async-start(), calls=%async_computation.11 | async-start | bytes 4718592 | tf_op jit(solution)/shard_map/reduce_scatter | solution.py:210
  166.8 109.9 %copy-start.4 = (bf16[512,512]{1,0:T(8,128)(2,1)}, bf16[512,512]{1,0:T(8,128)(2,1)S(1)}, u32[]{:S(2)}) copy-start(bf16[512,512]{1,0:T(8,128)(2,1)S(1)} %all_gather.23) | copy-start | bytes 1572868
  224.0 51.9 %copy-start.14 = (bf16[1,256,8,64]{1,3,2,0:T(8,128)(2,1)}, bf16[1,256,8,64]{1,3,2,0:T(8,128)(2,1)S(1)}, u32[]{:S(2)}) copy-start(bf16[1,256,8,64]{1,3,2,0:T(8,128)(2,1)S(1)} %convert_element_type.242) | copy-start | bytes 786436
  252.3 23.6 %copy-start.56 = (f32[512]{0:T(512)S(1)}, f32[512]{0:T(512)}, u32[]{:S(2)}) copy-start(f32[512]{0:T(512)} %convert_element_type.234) | copy-start | bytes 6148
  297.6 5.8 copy-start.10
  346.6 99.5 %reduce-scatter.12.cloned.1.call-start = ((), (), s32[]{:S(2)}) async-start(), calls=%async_computation.10 | async-start | bytes 4718592 | tf_op jit(solution)/shard_map/reduce_scatter | solution.py:210
  349.2 5.9 copy-start.43
  360.3 5.9 copy-start.43
  371.3 5.9 copy-start.43
  382.3 5.9 copy-start.43
  393.4 186.8 %reduce-scatter.24.cloned.1.call-start = ((), (), s32[]{:S(2)}) async-start(), calls=%async_computation.18 | async-start | bytes 270336
  394.4 51.7 %copy-start.20 = (bf16[256,512]{1,0:T(8,128)(2,1)}, bf16[256,512]{1,0:T(8,128)(2,1)S(1)}, u32[]{:S(2)}) copy-start(bf16[256,512]{1,0:T(8,128)(2,1)S(1)} %copy.111) | copy-start | bytes 786436
  396.9 51.5 %copy-start.15 = (bf16[1,256,8,64]{1,3,2,0:T(8,128)(2,1)S(1)}, bf16[1,256,8,64]{1,3,2,0:T(8,128)(2,1)}, u32[]{:S(2)}) copy-start(bf16[1,256,8,64]{1,3,2,0:T(8,128)(2,1)} %copy-done.14) | copy-start | bytes 786436
  448.3 265.9 %reduce-scatter.16.cloned.1.call-start = ((), (), s32[]{:S(2)}) async-start(), calls=%async_computation.12 | async-start | bytes 1081344 | tf_op jit(solution)/shard_map/reduce_scatter | solution.py:234
  450.7 404.9 %reduce-scatter.20.cloned.1.call-start = ((), (), s32[]{:S(2)}) async-start(), calls=%async_computation.14 | async-start | bytes 4325376 | tf_op jit(solution)/shard_map/reduce_scatter | solution.py:236
  457.7 540.4 %reduce-scatter.18.cloned.1.call-start = ((), (), s32[]{:S(2)}) async-start(), calls=%async_computation.13 | async-start | bytes 4325376 | tf_op jit(solution)/shard_map/reduce_scatter | solution.py:235
  462.5 639.6 %reduce-scatter.22.cloned.1.call-start = ((), (), s32[]{:S(2)}) async-start(), calls=%async_computation.17 | async-start | bytes 3244032
  468.0 42.6 %copy-start.47 = (bf16[256,512]{1,0:T(8,128)(2,1)S(1)}, bf16[256,512]{1,0:T(8,128)(2,1)}, u32[]{:S(2)}) copy-start(bf16[256,512]{1,0:T(8,128)(2,1)} %get-tuple-element.1183) | copy-start | bytes 786436
  468.0 42.6 %copy-start.48 = (bf16[256,512]{1,0:T(8,128)(2,1)S(1)}, bf16[256,512]{1,0:T(8,128)(2,1)}, u32[]{:S(2)}) copy-start(bf16[256,512]{1,0:T(8,128)(2,1)} %get-tuple-element.1188) | copy-start | bytes 786436
  468.0 43.4 %copy-start.22 = (bf16[256,512]{1,0:T(8,128)(2,1)S(1)}, bf16[256,512]{1,0:T(8,128)(2,1)}, u32[]{:S(2)}) copy-start(bf16[256,512]{1,0:T(8,128)(2,1)} %copy-done.20) | copy-start | bytes 786436
  468.0 43.4 %copy-start.39 = (bf16[1,256,1024]{2,1,0:T(8,128)(2,1)S(1)}, bf16[1,256,1024]{2,1,0:T(8,128)(2,1)}, u32[]{:S(2)}) copy-start(bf16[1,256,1024]{2,1,0:T(8,128)(2,1)} %reduce-scatter.12.cloned.1.call-done) | copy-start | bytes 1572868
  468.0 43.4 %copy-start.53 = (f32[256,512]{1,0:T(8,128)S(1)}, f32[256,512]{1,0:T(8,128)}, u32[]{:S(2)}) copy-start(f32[256,512]{1,0:T(8,128)} %copy-done.52) | copy-start | bytes 1572868
  (59 other events, 140.3 us)
Sparse Core Ops, SparseCore 0:
  11.0 57.8 all-gather.8
  72.0 47.2 all-gather.16
  120.9 50.0 all-gather.14
  173.7 55.4 all-gather.10
  232.0 55.3 all-gather.12
  346.7 48.8 reduce-scatter.13
  397.9 48.1 reduce-scatter.11
  448.5 131.6 reduce-scatter.23
  583.1 131.1 reduce-scatter.15
  716.9 138.6 reduce-scatter.19
  858.5 139.5 reduce-scatter.17
  1004.0 98.1 reduce-scatter.21
where the time goes:
time: 1120 us; the launch traced here: 1110 us
  waiting for transfers between devices  658 us (59%)
  blocking collectives  168 us (15%)
  local copies, waits for them, and re-layouts  113 us (10%)
  matrix products  113 us (10%)
  other arithmetic  36.6 us (3%)
  between operations  18 us (2%)
    unnamed x14, waiting for transfers between devices  171 us
    reduce_scatter x1, waiting for transfers between devices, body(): lax.psum_scatter(accum_grads[2], ('dp', 'seq'), scatter_dimension=0, tile...  142 us
    reduce_scatter x1, waiting for transfers between devices, body(): lax.psum_scatter(accum_grads[3], ('dp', 'seq'), scatter_dimension=0, tile...  141 us
    reduce_scatter x1, waiting for transfers between devices, body(): lax.psum_scatter(accum_grads[1], ('dp', 'seq'), scatter_dimension=0, tile...  133 us
    unnamed x2, blocking collectives  79.7 us
    reduce_scatter x2, waiting for transfers between devices, body(): lax.psum_scatter(kv_terms.astype(jnp.bfloat16), 'seq', scatter_dimension=...  50.1 us
    all_gather x1, blocking collectives, body(): lax.all_gather(params[1], ('dp', 'seq'), axis=0, tiled=True)  45.3 us
    all_gather x1, blocking collectives, body(): lax.all_gather(params[4], ('dp', 'seq'), axis=1, tiled=True)  43.2 us
  transfers between devices with their start and end apart: 12, of which 9 were waited for; matrix products, arithmetic and copies ran while one was open for 17% of the time, Pallas kernels for 0%

commit v1 on v0

v1 whole, which is shorter than its diff:
```python
import functools
import math

import jax
import jax.numpy as jnp
from jax import lax
from jax.experimental import pallas as pl
from jax.experimental.pallas import tpu as pltpu
from jax.sharding import Mesh, PartitionSpec as P

D = 512
HEADS = 8
HEAD_DIM = 64
FF = 2048
BLOCK = 256
HALF = D // 2
CORE_HEADS = HEADS // 2
SLABS = FF // D
BF = jnp.bfloat16
F32 = jnp.float32
MESH_AXES = ("a", "b", "z", "c")
VMEM = pl.BlockSpec(memory_space=pltpu.VMEM)
SMEM = pl.BlockSpec(memory_space=pltpu.SMEM)
ANY = pl.BlockSpec(memory_space=pl.ANY)
GELU_C = math.sqrt(2.0 / math.pi)


def dot(left, right):
    return jnp.dot(left, right, preferred_element_type=F32)


def ndot(left, right):
    return lax.dot_general(left, right, (((1,), (1,)), ((), ())), preferred_element_type=F32)


def tdot(left, right):
    return lax.dot_general(left, right, (((0,), (0,)), ((), ())), preferred_element_type=F32)


def flip(block):
    return block.astype(F32).T.astype(BF)


def query_blocks(z, c, nz):
    half = nz // 2
    k = lax.rem(z, half)

    def first(parity):
        return jnp.where(lax.rem(k, 2) == parity, k, nz - 1 - k)

    mine, other = first(c), first(1 - c)
    return (mine, mine + nz, other, other + nz)


def attend_kernel(nz, n1, n2, *refs):
    ids = refs[0]
    xo = refs[1 : 1 + nz]
    xs = refs[1 + nz : 1 + 2 * nz]
    pieces = refs[1 + 2 * nz : 1 + 2 * nz + 2 * n1 * n2]
    bias_q, bias_v = refs[1 + 2 * nz + 2 * n1 * n2 : 3 + 2 * nz + 2 * n1 * n2]
    (xall, wq, kn, vn, qn, ot, lse, o_mine, o_send, x_mine) = refs[
        3 + 2 * nz + 2 * n1 * n2 : 13 + 2 * nz + 2 * n1 * n2
    ]
    vt, qz, m_s, l_s, acc_s = refs[13 + 2 * nz + 2 * n1 * n2 :]
    z, c, a, b = ids[0], ids[1], ids[2], ids[3]
    for r in range(nz):
        src = lax.rem(z - r + nz, nz)
        xall[2 * src + c] = xo[r][...]
        xall[2 * src + 1 - c] = xs[r][...]
    i = 0
    for h in range(2):
        for ra in range(n1):
            for rb in range(n2):
                dp = lax.rem(a - ra + n1, n1) * n2 + lax.rem(b - rb + n2, n2)
                wq[2 * dp + h] = pieces[i][...]
                i += 1
    weights = wq.shape[0] * wq.shape[1]
    w_all = wq[...].reshape(weights, 3 * HALF)
    w_q, w_kv = w_all[:, :HALF], w_all[:, HALF:]

    def project(block, unused):
        kv = dot(xall[block], w_kv)
        kn[block] = kv[:, :HALF].astype(BF)
        value = kv[:, HALF:] + bias_v[...]
        vn[block] = value.astype(BF)
        vt[block] = value.T.astype(BF)
        return unused

    lax.fori_loop(0, 2 * nz, project, 0)
    blocks = query_blocks(z, c, nz)
    rows = lax.broadcasted_iota(jnp.int32, (HALF, BLOCK), 0) // HEAD_DIM
    for i, block in enumerate(blocks):
        xq = xall[block]
        if i < 2:
            x_mine[i] = xq
        q = ((dot(xq, w_q) + bias_q[...]).astype(BF).astype(F32) * (1.0 / math.sqrt(HEAD_DIM))).astype(BF)
        qn[i] = q
        qt = q.astype(F32).T
        for h in range(CORE_HEADS):
            qz[h] = jnp.where(rows == h, qt, 0.0).astype(BF)
        m_s[...] = jnp.full_like(m_s, -1e30)
        l_s[...] = jnp.zeros_like(l_s)
        acc_s[...] = jnp.zeros_like(acc_s)

        def step(kb, unused):
            keys = kn[kb]
            for h in range(CORE_HEADS):
                head = slice(h * HEAD_DIM, (h + 1) * HEAD_DIM)
                s = dot(keys, qz[h])
                old = m_s[h]
                new = jnp.maximum(old, jnp.max(s, axis=0, keepdims=True))
                p = jnp.exp(s - new)
                shrink = jnp.exp(old - new)
                m_s[h] = new
                l_s[h] = l_s[h] * shrink + jnp.sum(p, axis=0, keepdims=True)
                acc_s[head, :] = acc_s[head, :] * shrink + dot(vt[kb, head, :], p.astype(BF))
            return unused

        lax.fori_loop(0, block + 1, step, 0)
        for h in range(CORE_HEADS):
            head = slice(h * HEAD_DIM, (h + 1) * HEAD_DIM)
            total = l_s[h]
            lse[i, h : h + 1, :] = m_s[h] + jnp.log(total)
            acc_s[head, :] = acc_s[head, :] / total
        o = acc_s[...]
        ot[i] = o
        target = o_mine if i < 2 else o_send
        target[i % 2] = o.T.astype(BF)


def ffn_kernel(n1, n2, *refs):
    npieces = 2 * n1 * n2
    ids, alphas, o_mine, o_recv, x_mine, cot_a, cot_b, bo, bi, bb = refs[:10]
    pieces = refs[10 : 10 + 2 * npieces]
    (out, dx1, d_mine, d_send, g_keep, g_send, gb_o, gb_i, gb_b, ga) = refs[
        10 + 2 * npieces : 20 + 2 * npieces
    ]
    w, wo_s, wi_s, wb_s, mixed, h_s, r_s, dpre_s, dff_s, dattn_s, g_s, sems = refs[20 + 2 * npieces :]
    c, a, b, group = ids[1], ids[2], ids[3], ids[4]
    copies = []
    i = 0
    for h in range(2):
        for ra in range(n1):
            for rb in range(n2):
                dp = lax.rem(a - ra + n1, n1) * n2 + lax.rem(b - rb + n2, n2)
                for own in range(2):
                    copies.append(
                        pltpu.make_async_copy(
                            pieces[own * npieces + i],
                            w.at[c if own == 0 else 1 - c, 2 * dp + h],
                            sems.at[own * npieces + i],
                        )
                    )
                i += 1
    for copy in copies:
        copy.start()
    mixed[c] = o_mine[...].reshape(2 * BLOCK, HALF)
    mixed[1 - c] = o_recv[...].reshape(2 * BLOCK, HALF)
    for copy in copies:
        copy.wait()
    ndp = n1 * n2
    rd = D // ndp
    for half in range(2):
        lanes = slice(half * HALF, (half + 1) * HALF)
        whole = w[half].reshape(ndp, 9 * rd, HALF)
        wb_s[:, lanes] = whole[:, : 4 * rd].reshape(FF, HALF)
        for s in range(SLABS):
            wi_s[s, :, lanes] = whole[:, (4 + s) * rd : (5 + s) * rd].reshape(D, HALF)
        wo_s[:, lanes] = whole[:, 8 * rd :].reshape(D, HALF)
    alpha_attn, alpha_ffn = alphas[0], alphas[1]

    def tile(t, sums):
        rows = pl.ds(pl.multiple_of(t * BLOCK, BLOCK), BLOCK)
        ob0, ob1 = mixed[0, rows, :], mixed[1, rows, :]
        attn = dot(ob0, wo_s[:HALF, :]) + dot(ob1, wo_s[HALF:, :]) + bo[...]
        x1 = x_mine[t].astype(F32) + alpha_attn * attn
        hidden = x1.astype(BF)
        h_s[rows, :] = hidden
        dy = jnp.where(t == group, cot_a[...], cot_b[...]).astype(F32)
        dff = (alpha_ffn * dy).astype(BF)
        dff_s[rows, :] = dff
        ff = jnp.zeros((BLOCK, D), F32) + bb[...]
        dx = dy
        for s in range(SLABS):
            lanes = slice(s * D, (s + 1) * D)
            pre = dot(hidden, wi_s[s]) + bi[:, lanes]
            square = pre * pre
            t_ = jnp.tanh(GELU_C * pre * (1.0 + 0.044715 * square))
            half_up = 0.5 * (1.0 + t_)
            r = (pre * half_up).astype(BF)
            slope = half_up + 0.5 * pre * (1.0 - t_ * t_) * (GELU_C * (1.0 + 3.0 * 0.044715 * square))
            r_s[rows, lanes] = r
            ff = ff + dot(r, wb_s[lanes, :])
            dr = ndot(dff, wb_s[lanes, :]).astype(BF).astype(F32)
            dpre = (dr * slope).astype(BF)
            dpre_s[rows, lanes] = dpre
            dx = dx + ndot(dpre, wi_s[s])
        out[t] = (x1 + alpha_ffn * ff).astype(BF)
        dx1[t] = dx
        dattn = (alpha_attn * dx).astype(BF)
        dattn_s[rows, :] = dattn
        d_mixed = ndot(dattn, wo_s[...]).astype(BF)
        d_mine[t] = jnp.where(c == 0, d_mixed[:, :HALF], d_mixed[:, HALF:])
        d_send[t] = jnp.where(c == 0, d_mixed[:, HALF:], d_mixed[:, :HALF])
        return (sums[0] + jnp.sum(dx * attn, axis=0, keepdims=True), sums[1] + jnp.sum(dy * ff, axis=0, keepdims=True))

    zero = jnp.zeros((1, D), F32)
    sum_attn, sum_ffn = lax.fori_loop(0, 2, tile, (zero, zero))
    ga[...] = jnp.concatenate([sum_attn, sum_ffn], axis=0)
    dff, dattn, hidden = dff_s[...], dattn_s[...], h_s[...]
    gb_o[...] = jnp.sum(dattn.astype(F32), axis=0, keepdims=True)
    gb_b[...] = jnp.sum(dff.astype(F32), axis=0, keepdims=True)
    ht = flip(hidden)

    def put(first, value):
        count = value.shape[0] // ndp
        for half in range(2):
            part = value[:, half * HALF : (half + 1) * HALF].astype(BF).reshape(ndp, count, HALF)
            g_s[half, :, first : first + count, :] = part

    for s in range(SLABS):
        lanes = slice(s * D, (s + 1) * D)
        dpre = dpre_s[:, lanes]
        gb_i[:, lanes] = jnp.sum(dpre.astype(F32), axis=0, keepdims=True)
        put((4 + s) * rd, dot(ht, dpre))
        g_back = dot(flip(r_s[:, lanes]), dff)
        per = ndp // SLABS if ndp >= SLABS else 1
        count = 4 * rd
        for half in range(2):
            part = g_back[:, half * HALF : (half + 1) * HALF].astype(BF).reshape(per, count, HALF)
            g_s[half, s * per : (s + 1) * per, :count, :] = part
    both = jnp.concatenate([mixed[0], mixed[1]], axis=1)
    put(8 * rd, dot(flip(both), dattn))
    done = [
        pltpu.make_async_copy(g_s.at[c], g_keep, sems.at[0]),
        pltpu.make_async_copy(g_s.at[1 - c], g_send, sems.at[1]),
    ]
    for copy in done:
        copy.start()
    for copy in done:
        copy.wait()


def back_kernel(nz, *refs):
    (ids, xall, wq, kn, vn, qn, ot, lse, d_mine, d_recv, dx1) = refs[:11]
    dx_keep, dx_send, dw, gb = refs[11:15]
    kt, qz, qzt, oz, ozt, dk_s, dv_s, dq_s, dqkv, dxs = refs[15:]
    z, c = ids[0], ids[1]
    scale = 1.0 / math.sqrt(HEAD_DIM)
    dk_s[...] = jnp.zeros_like(dk_s)
    dv_s[...] = jnp.zeros_like(dv_s)
    dqkv[...] = jnp.zeros_like(dqkv)

    def turn(block, unused):
        kt[block] = flip(kn[block])
        return unused

    lax.fori_loop(0, 2 * nz, turn, 0)
    rows = lax.broadcasted_iota(jnp.int32, (HALF, BLOCK), 0) // HEAD_DIM
    lanes = lax.broadcasted_iota(jnp.int32, (BLOCK, HALF), 1) // HEAD_DIM
    blocks = query_blocks(z, c, nz)
    gq = jnp.zeros((1, HALF), F32)
    for i, block in enumerate(blocks):
        q = qn[i].astype(F32)
        d_o = (d_mine[i] if i < 2 else d_recv[i - 2]).astype(F32)
        qt, dot_ = q.T, d_o.T
        product = dot_ * ot[i]
        deltas = []
        for h in range(CORE_HEADS):
            head = slice(h * HEAD_DIM, (h + 1) * HEAD_DIM)
            deltas.append(jnp.sum(product[head], axis=0, keepdims=True))
            qz[h] = jnp.where(lanes == h, q, 0.0).astype(BF)
            oz[h] = jnp.where(lanes == h, d_o, 0.0).astype(BF)
            qzt[h] = jnp.where(rows == h, qt, 0.0).astype(BF)
            ozt[h] = jnp.where(rows == h, dot_, 0.0).astype(BF)
        dq_s[...] = jnp.zeros_like(dq_s)

        def step(kb, unused):
            keys, values = kn[kb], vn[kb]
            dk = dk_s[kb]
            dv = dv_s[kb]
            for h in range(CORE_HEADS):
                head = slice(h * HEAD_DIM, (h + 1) * HEAD_DIM)
                p = jnp.exp(dot(keys, qzt[h]) - lse[i, h : h + 1, :])
                dp = dot(values, ozt[h])
                ds = (p * (dp - deltas[h])).astype(BF)
                dv = dv + dot(p.astype(BF), oz[h])
                dk = dk + dot(ds, qz[h])
                dq_s[head, :] = dq_s[head, :] + dot(kt[kb, head, :], ds)
            dk_s[kb] = dk
            dv_s[kb] = dv
            return unused

        lax.fori_loop(0, block + 1, step, 0)
        dq = (dq_s[...] * scale).T.astype(BF)
        gq = gq + jnp.sum(dq.astype(F32), axis=0, keepdims=True)
        dqkv[block, :, :HALF] = dq

    w_all = wq[...].reshape(D, 3 * HALF)

    def finish(block, gv):
        dv = dv_s[block].astype(BF)
        dqkv[block, :, HALF : 2 * HALF] = dk_s[block].astype(BF)
        dqkv[block, :, 2 * HALF :] = dv
        dxs[block] = ndot(dqkv[block], w_all)
        return gv + jnp.sum(dv.astype(F32), axis=0, keepdims=True)

    gv = lax.fori_loop(0, 2 * nz, finish, jnp.zeros((1, HALF), F32))
    gb[...] = jnp.concatenate([gq, gv], axis=0)
    for i in range(2):
        dxs[blocks[i]] = dxs[blocks[i]] + dx1[i]
    for s in range(nz):
        dx_keep[s] = dxs[2 * s + c].astype(BF)
        dx_send[s] = dxs[2 * s + 1 - c].astype(BF)
    total = jnp.zeros((D, 3 * HALF), F32)
    acc = dot(flip(xall[0]), dqkv[0])
    for block in range(1, 2 * nz):
        acc = acc + dot(flip(xall[block]), dqkv[block])
    dw[...] = (total + acc).astype(BF)


def shape(dims, kind):
    return jax.ShapeDtypeStruct(dims, kind)


def cost(flops, size, trans=0):
    return pl.CostEstimate(flops=int(flops), bytes_accessed=int(size), transcendentals=int(trans))


def make_body(n1, n2, nz):
    ndp = n1 * n2
    nsh = ndp * nz * 2
    rs = D // nsh
    rd = D // ndp
    half = nz // 2
    swap = [(0, 1), (1, 0)]

    def turn(count, by):
        return [(s, (s + by) % count) for s in range(count)]

    def place(k, c):
        return (k if k % 2 == c else nz - 1 - k) // 2

    near, far = [], []
    for k in range(half):
        for c in range(2):
            src = place(k, c)
            near += [(2 * src + c, 2 * k + c), (2 * (half + src) + c, 2 * (half + k) + c)]
            far += [(2 * (half + src) + c, 2 * k + c), (2 * src + c, 2 * (half + k) + c)]
    near_back = [(d, s) for s, d in near]
    far_back = [(d, s) for s, d in far]

    def pick(array, index, axis=0):
        return lax.dynamic_index_in_dim(array, index, axis, keepdims=False)

    def body(inputs, w_qkv, bias_qv, w_out, bias_out, w_in, bias_in, w_back, bias_back, alphas, cotangent):
        z, c = lax.axis_index("z"), lax.axis_index("c")
        a, b = lax.axis_index("a"), lax.axis_index("b")
        group = z // half
        ids = jnp.stack([z, c, a, b, group]).astype(jnp.int32)

        def by_core(own, other):
            return jnp.where(c == 0, jnp.stack([own, other]), jnp.stack([other, own]))

        def along_z(piece):
            parts = [piece] + [lax.ppermute(piece, "z", turn(nz, r)) for r in range(1, nz)]
            ring = jnp.stack(parts[::-1] + parts[::-1])
            return lax.dynamic_slice_in_dim(ring, nz - 1 - z, nz, 0)

        def along_dp(rows):
            cut = rows.shape[0] // 2
            first, second = rows[:cut], rows[cut:]
            f1 = [first] + [lax.ppermute(first, "b", turn(n2, r)) for r in range(1, n2)]
            s1 = [second] + [lax.ppermute(second, "a", turn(n1, r)) for r in range(1, n1)]
            parts = []
            for ra in range(n1):
                for rb in range(n2):
                    parts.append(f1[rb] if ra == 0 else lax.ppermute(f1[rb], "a", turn(n1, ra)))
            for ra in range(n1):
                for rb in range(n2):
                    parts.append(s1[ra] if rb == 0 else lax.ppermute(s1[ra], "b", turn(n2, rb)))
            return parts

        def scatter_dp(whole):
            w5 = whole.reshape((n1, n2) + whole.shape[1:])
            first, second = w5[:, :, 0], w5[:, :, 1]

            def over(part, name, count, me, axis):
                got = [
                    lax.ppermute(pick(part, lax.rem(me + r, count), axis), name, turn(count, r))
                    for r in range(1, count)
                ]
                total = pick(part, me, axis).astype(F32)
                for g in got:
                    total = total + g.astype(F32)
                return total.astype(BF)

            first = over(first, "b", n2, b, 1)
            second = over(second, "a", n1, a, 0)
            first = over(first, "a", n1, a, 0)
            second = over(second, "b", n2, b, 0)
            return first, second

        def scatter_z(parts):
            got = [
                lax.ppermute(pick(parts, lax.rem(z + r, nz)), "z", turn(nz, r)) for r in range(1, nz)
            ]
            total = pick(parts, z).astype(F32)
            for g in got:
                total = total + g.astype(F32)
            return total

        wq_cut = w_qkv.reshape(rs, 3, 2, HALF)
        wq_own = pick(wq_cut, c, 2).reshape(rs, 3 * HALF)
        wq_give = pick(wq_cut, 1 - c, 2).reshape(rs, 3 * HALF)
        wq_chip = by_core(wq_own, lax.ppermute(wq_give, "c", swap)).reshape(2 * rs, 3 * HALF)
        wq_pieces = along_dp(along_z(wq_chip).reshape(rd, 3 * HALF))

        x_own = [pick(inputs, group)] + [
            lax.ppermute(pick(inputs, lax.rem(z + r, nz) // half), "z", turn(nz, r)) for r in range(1, nz)
        ]
        x_other = [lax.ppermute(part, "c", swap) for part in x_own]

        def columns(which):
            back = pick(w_back.reshape(4 * rs, 2, HALF), which, 1)
            win = pick(w_in.reshape(rs, SLABS, 2, HALF), which, 2)
            win = jnp.transpose(win, (1, 0, 2)).reshape(SLABS * rs, HALF)
            return jnp.concatenate([back, win, pick(w_out.reshape(rs, 2, HALF), which, 1)], axis=0)

        wf_chip = by_core(columns(c), lax.ppermute(columns(1 - c), "c", swap))
        wf = along_z(wf_chip)
        wf = jnp.concatenate(
            [wf[:, :, : 4 * rs].reshape(4 * rd, HALF)]
            + [wf[:, :, (4 + s) * rs : (5 + s) * rs].reshape(rd, HALF) for s in range(SLABS)]
            + [wf[:, :, 8 * rs :].reshape(rd, HALF)],
            axis=0,
        )
        wf_pieces = along_dp(wf)
        wf_others = [lax.ppermute(part, "c", swap) for part in wf_pieces]

        small = jnp.concatenate([bias_qv[0], bias_qv[1], bias_out, bias_back, bias_in])
        small = lax.all_to_all(
            jnp.broadcast_to(small[None], (nsh, 8 * rs)), MESH_AXES, 0, 0, tiled=True
        ).astype(F32)
        bias_q = pick(small[:, :rs].reshape(2, 1, HALF), c)
        bias_v = pick(small[:, rs : 2 * rs].reshape(2, 1, HALF), c)
        bo = small[:, 2 * rs : 3 * rs].reshape(1, D)
        bb = small[:, 3 * rs : 4 * rs].reshape(1, D)
        bi = small[:, 4 * rs :].reshape(1, FF)

        cot_a = lax.ppermute(pick(cotangent, group), ("z", "c"), near)
        cot_b = lax.ppermute(pick(cotangent, 1 - group), ("z", "c"), far)

        nb = 2 * nz
        pairs = (2 * nb + 2) * CORE_HEADS * BLOCK * BLOCK
        (xall, wq, kn, vn, qn, ot, lse, o_mine, o_send, x_mine) = pl.pallas_call(
            functools.partial(attend_kernel, nz, n1, n2),
            out_shape=(
                shape((nb, BLOCK, D), BF),
                shape((2 * ndp, rd // 2, 3 * HALF), BF),
                shape((nb, BLOCK, HALF), BF),
                shape((nb, BLOCK, HALF), BF),
                shape((4, BLOCK, HALF), BF),
                shape((4, HALF, BLOCK), F32),
                shape((4, CORE_HEADS, BLOCK), F32),
                shape((2, BLOCK, HALF), BF),
                shape((2, BLOCK, HALF), BF),
                shape((2, BLOCK, D), BF),
            ),
            in_specs=[SMEM] + [VMEM] * (2 * nz + 2 * ndp + 2),
            out_specs=(VMEM,) * 10,
            scratch_shapes=[
                pltpu.VMEM((nb, HALF, BLOCK), BF),
                pltpu.VMEM((CORE_HEADS, HALF, BLOCK), BF),
                pltpu.VMEM((CORE_HEADS, 1, BLOCK), F32),
                pltpu.VMEM((CORE_HEADS, 1, BLOCK), F32),
                pltpu.VMEM((HALF, BLOCK), F32),
            ],
            compiler_params=pltpu.CompilerParams(vmem_limit_bytes=40 * 2**20),
            cost_estimate=cost(16 * pairs * HALF // 4, 8 * 2**20, pairs),
            name="attend",
        )(ids, *x_own, *x_other, *wq_pieces, bias_q, bias_v)
        o_recv = lax.ppermute(o_send, "c", swap)

        npieces = 2 * ndp
        nh = 9 * rd // 2
        (out, dx1, d_mine, d_send, g_keep, g_send, gb_o, gb_i, gb_b, ga) = pl.pallas_call(
            functools.partial(ffn_kernel, n1, n2),
            out_shape=(
                shape((2, BLOCK, D), BF),
                shape((2, BLOCK, D), F32),
                shape((2, BLOCK, HALF), BF),
                shape((2, BLOCK, HALF), BF),
                shape((ndp, 9 * rd, HALF), BF),
                shape((ndp, 9 * rd, HALF), BF),
                shape((1, D), F32),
                shape((1, FF), F32),
                shape((1, D), F32),
                shape((2, D), F32),
            ),
            in_specs=[SMEM, SMEM] + [VMEM] * 8 + [ANY] * (2 * npieces),
            out_specs=(VMEM,) * 4 + (ANY, ANY) + (VMEM,) * 4,
            scratch_shapes=[
                pltpu.VMEM((2, 2 * ndp, nh, HALF), BF),
                pltpu.VMEM((D, D), BF),
                pltpu.VMEM((SLABS, D, D), BF),
                pltpu.VMEM((FF, D), BF),
                pltpu.VMEM((2, 2 * BLOCK, HALF), BF),
                pltpu.VMEM((2 * BLOCK, D), BF),
                pltpu.VMEM((2 * BLOCK, FF), BF),
                pltpu.VMEM((2 * BLOCK, FF), BF),
                pltpu.VMEM((2 * BLOCK, D), BF),
                pltpu.VMEM((2 * BLOCK, D), BF),
                pltpu.VMEM((2, ndp, 9 * rd, HALF), BF),
                pltpu.SemaphoreType.DMA((2 * npieces,)),
            ],
            compiler_params=pltpu.CompilerParams(vmem_limit_bytes=48 * 2**20),
            cost_estimate=cost(6 * 2 * BLOCK * 9 * D * HALF * 2, 20 * 2**20, 2 * BLOCK * FF),
            name="ffn",
        )(ids, alphas, o_mine, o_recv, x_mine, cot_a, cot_b, bo, bi, bb, *wf_pieces, *wf_others)
        d_recv = lax.ppermute(d_send, "c", swap)

        out_a = lax.ppermute(pick(out, group), ("z", "c"), near_back)
        out_b = lax.ppermute(pick(out, 1 - group), ("z", "c"), far_back)
        outputs = jnp.where(group == 0, jnp.stack([out_a, out_b]), jnp.stack([out_b, out_a]))

        g_all = (g_keep.astype(F32) + lax.ppermute(g_send, "c", swap).astype(F32)).astype(BF)
        g_first, g_second = scatter_dp(g_all.reshape(ndp, 2, nh, HALF))
        g_dp = jnp.concatenate([g_first, g_second], axis=0)
        g_z = jnp.concatenate(
            [g_dp[: 4 * rd].reshape(nz, 2, 4 * rs, HALF)]
            + [g_dp[(4 + s) * rd : (5 + s) * rd].reshape(nz, 2, rs, HALF) for s in range(SLABS)]
            + [g_dp[8 * rd :].reshape(nz, 2, rs, HALF)],
            axis=2,
        )
        g_mine = scatter_z(g_z)
        g_own = pick(g_mine, c)
        g_other = lax.ppermute(pick(g_mine, 1 - c).astype(BF), "c", swap).astype(F32)
        g_whole = by_core(g_own, g_other)
        grad_w_back = jnp.transpose(g_whole[:, : 4 * rs], (1, 0, 2)).reshape(4 * rs, D)
        grad_w_in = jnp.transpose(
            g_whole[:, 4 * rs : 8 * rs].reshape(2, SLABS, rs, HALF), (2, 1, 0, 3)
        ).reshape(rs, FF)
        grad_w_out = jnp.transpose(g_whole[:, 8 * rs :], (1, 0, 2)).reshape(rs, D)

        dx_keep, dx_send, dw, gb = pl.pallas_call(
            functools.partial(back_kernel, nz),
            out_shape=(
                shape((nz, BLOCK, D), BF),
                shape((nz, BLOCK, D), BF),
                shape((D, 3 * HALF), BF),
                shape((2, HALF), F32),
            ),
            in_specs=[SMEM] + [VMEM] * 10,
            out_specs=(VMEM,) * 4,
            scratch_shapes=[
                pltpu.VMEM((nb, HALF, BLOCK), BF),
                pltpu.VMEM((CORE_HEADS, BLOCK, HALF), BF),
                pltpu.VMEM((CORE_HEADS, HALF, BLOCK), BF),
                pltpu.VMEM((CORE_HEADS, BLOCK, HALF), BF),
                pltpu.VMEM((CORE_HEADS, HALF, BLOCK), BF),
                pltpu.VMEM((nb, BLOCK, HALF), F32),
                pltpu.VMEM((nb, BLOCK, HALF), F32),
                pltpu.VMEM((HALF, BLOCK), F32),
                pltpu.VMEM((nb, BLOCK, 3 * HALF), BF),
                pltpu.VMEM((nb, BLOCK, D), F32),
            ],
            compiler_params=pltpu.CompilerParams(vmem_limit_bytes=56 * 2**20),
            cost_estimate=cost(40 * pairs * HALF // 4, 12 * 2**20, pairs),
            name="back",
        )(ids, xall, wq, kn, vn, qn, ot, lse, d_mine, d_recv, dx1)

        dx = (dx_keep.astype(F32) + lax.ppermute(dx_send, "c", swap).astype(F32)).astype(BF)
        parts = [pick(dx, z)] + [
            lax.ppermute(pick(dx, lax.rem(z + r, nz)), "z", turn(nz, r)) for r in range(1, nz)
        ]
        grads = []
        for which in range(2):
            total = jnp.zeros((BLOCK, D), F32)
            for r, part in enumerate(parts):
                source = lax.rem(z - r + nz, nz) // half
                total = total + jnp.where(source == which, part.astype(F32), 0.0)
            grads.append(total.astype(BF))
        grad_inputs = jnp.stack(grads)

        first, second = scatter_dp(dw.reshape(ndp, 2, rd // 2, 3 * HALF))
        dw_z = jnp.concatenate([first, second], axis=0).reshape(nz, 2, rs, 3 * HALF)
        dw_mine = scatter_z(dw_z)
        dw_own = pick(dw_mine, c)
        dw_other = lax.ppermute(pick(dw_mine, 1 - c).astype(BF), "c", swap).astype(F32)
        grad_w_qkv = jnp.transpose(
            by_core(dw_own, dw_other).reshape(2, rs, 3, HALF), (1, 2, 0, 3)
        ).reshape(rs, 3 * D)

        at = jnp.arange(2, dtype=jnp.int32)[:, None] == c
        gq = jnp.where(at, gb[0][None], 0.0).reshape(nsh, rs)
        gv = jnp.where(at, gb[1][None], 0.0).reshape(nsh, rs)
        gate = jnp.broadcast_to(jnp.sum(ga, axis=1)[None], (nsh, 2))
        packed = jnp.concatenate(
            [gq, gv, gb_o.reshape(nsh, rs), gb_b.reshape(nsh, rs), gb_i.reshape(nsh, 4 * rs), gate], axis=1
        )
        packed = jnp.sum(lax.all_to_all(packed, MESH_AXES, 0, 0, tiled=True), axis=0)
        grad_bias_qv = packed[: 2 * rs].reshape(2, rs)
        return (
            outputs,
            grad_inputs,
            grad_w_qkv,
            grad_bias_qv,
            grad_w_out,
            packed[2 * rs : 3 * rs],
            grad_w_in,
            packed[4 * rs : 8 * rs],
            grad_w_back,
            packed[3 * rs : 4 * rs],
            packed[8 * rs :],
        )

    return body


def solution(mesh):
    ndp, nseq = mesh.devices.shape
    n1 = math.isqrt(ndp)
    n2 = ndp // n1
    nz = nseq // 2
    fine = Mesh(mesh.devices.reshape(n1, n2, nz, 2), MESH_AXES)
    dp, seq = ("a", "b"), ("z", "c")
    rows = P(dp, seq, None)
    both = dp + seq
    return jax.shard_map(
        make_body(n1, n2, nz),
        mesh=fine,
        in_specs=(
            rows,
            P(both, None),
            P(None, both),
            P(both, None),
            P(both),
            P(both, None),
            P(both),
            P(both, None),
            P(both),
            P(),
            rows,
        ),
        out_specs=(
            rows,
            rows,
            P(both, None),
            P(None, both),
            P(both, None),
            P(both),
            P(both, None),
            P(both),
            P(both, None),
            P(both),
            P(),
        ),
        check_vma=False,
    )
```

time: 1120 us -> 309 us (0.28)
  waiting for transfers between devices: 658 us -> 89 us
  blocking collectives: 168 us -> 0 us
  matrix products: 113 us -> 0 us
  starting transfers between devices: 0.74 us -> 79.8 us
  Pallas kernels: 0 us -> 78.5 us
  local copies, waits for them, and re-layouts: 113 us -> 46.5 us
  other arithmetic: 36.6 us -> 11 us
  between operations: 18 us -> 1.67 us
    reduce_scatter x5 -> x0, waiting for transfers between devices: 467 us -> none  [the longest x1 142 us: body(): lax.psum_scatter(accum_grads[2], ('dp', 'seq'), scatter_dimension=0, tile...]
    unnamed x14 -> x0, waiting for transfers between devices: 171 us -> none
    dot_general x80 -> x0, matrix products: 113 us -> none  [the longest x8 21.9 us: value_update(): jnp.einsum('shqk,skhd->sqhd', probs.astype(jnp.bfloat16), values, preferr...]
    all_gather x2 -> x0, blocking collectives: 88.6 us -> none  [the longest x1 45.3 us: body(): lax.all_gather(params[1], ('dp', 'seq'), axis=0, tiled=True)]
    unnamed x2 -> x0, blocking collectives: 79.7 us -> none
    pallas_call x0 -> x3, Pallas kernels: none -> 78.5 us  [the longest x1 32.5 us: body(): pl.pallas_call(functools.partial(back_kernel, nz), out_shape=(shape((nz,...]
    ppermute x0 -> x62, waiting for transfers between devices: none -> 77.1 us  [the longest x6 22.3 us: along_z(): lax.ppermute(piece, 'z', turn(nz, r))]
    ppermute x0 -> x62, starting transfers between devices: none -> 70.9 us  [the longest x6 18.6 us: along_z(): lax.ppermute(piece, 'z', turn(nz, r))]
  transfers between devices with their start and end apart: 12 -> 64, of which waited for: 9 -> 28; matrix products, arithmetic and copies ran while one was open for 17% -> 9% of each run, Pallas kernels for 0% -> 20%
where the time goes in v1:
time: 309 us; the launch traced here: 306 us
  waiting for transfers between devices  89 us (29%)
  starting transfers between devices  79.8 us (26%)
  Pallas kernels  78.5 us (25%)
  local copies, waits for them, and re-layouts  46.5 us (15%)
  other arithmetic  11 us (4%)
    pallas_call x1, Pallas kernels, body(): pl.pallas_call(functools.partial(back_kernel, nz), out_shape=(shape((nz,...  32.5 us
    pallas_call x1, Pallas kernels, body(): pl.pallas_call(functools.partial(attend_kernel, nz, n1, n2), out_shape=(s...  28.4 us
    unnamed x121, local copies, waits for them, and re-layouts  25.7 us
    ppermute x6, waiting for transfers between devices, along_z(): lax.ppermute(piece, 'z', turn(nz, r))  22.3 us
    ppermute x8, waiting for transfers between devices, over(): lax.ppermute(pick(part, lax.rem(me + r, count), axis), name, turn(count, r))  19.1 us
    ppermute x6, starting transfers between devices, along_z(): lax.ppermute(piece, 'z', turn(nz, r))  18.6 us
    pallas_call x1, Pallas kernels, body(): pl.pallas_call(functools.partial(ffn_kernel, n1, n2), out_shape=(shape((2...  17.5 us
    ppermute x6, waiting for transfers between devices, scatter_z(): lax.ppermute(pick(parts, lax.rem(z + r, nz)), 'z', turn(nz, r))  12.3 us
  transfers between devices with their start and end apart: 64, of which 28 were waited for; matrix products, arithmetic and copies ran while one was open for 9% of the time, Pallas kernels for 20%

profile of v1, /device:TPU:0, one launch (start us, length us, event | category | flops | bytes accessed | tf_op | source)
XLA Modules:
  0.0 306.4 jit_solution(7828436008595080732)
XLA Ops:
  5.5 2.9 collective-permute-start
  8.4 2.6 collective-permute-start.1
  13.9 15.5 %collective-permute-done.8 = bf16[32,768]{1,0:T(8,128)(2,1)S(1)} collective-permute-done((bf16[32,768]{1,0:T(8,128)(2,1)S(1)}, bf16[32,768]{1,0:T(8,128)(2,1)S(1)}, u32[]{:S(2)}, u32[]{:S(2)}) %collective-permute-start.8) | collective-permute-done | bytes 49184 | tf_op jit(solution)/shard_map/ppermute | solution.py:366
  29.4 5.2 %collective-permute-start.9 = (bf16[32,768]{1,0:T(8,128)(2,1)S(1)}, bf16[32,768]{1,0:T(8,128)(2,1)S(1)}, u32[]{:S(2)}, u32[]{:S(2)}) collective-permute-start(bf16[32,768]{1,0:T(8,128)(2,1)S(1)} %bitcast.249), channel_id=1, source_target_pairs={{0,4},{2,6},{4,0},{6,2},{1,5},{3,7},{5,1},{7,3},{8,12},{10,14},{12... | collective-permute-start | bytes 147464 | tf_op jit(solution)/shard_map/ppermute | solution.py:366
  36.7 4.5 %collective-permute-start.21 = (bf16[2,144,256]{2,1,0:T(8,128)(2,1)S(1)}, bf16[2,144,256]{2,1,0:T(8,128)(2,1)S(1)}, u32[]{:S(2)}, u32[]{:S(2)}) collective-permute-start(bf16[2,144,256]{2,1,0:T(8,128)(2,1)S(1)} %maximum_select_fusion.2), channel_id=1, source_target_pairs={{0,6},{2,0},{4,2},{6,4},{1,7},{3,1},{5,3},{7,5},{8,14},{10,8},{12,... | collective-permute-start | bytes 442376 | tf_op jit(solution)/shard_map/ppermute | solution.py:366
  42.3 3.2 %collective-permute-done.21 = bf16[2,144,256]{2,1,0:T(8,128)(2,1)S(1)} collective-permute-done((bf16[2,144,256]{2,1,0:T(8,128)(2,1)S(1)}, bf16[2,144,256]{2,1,0:T(8,128)(2,1)S(1)}, u32[]{:S(2)}, u32[]{:S(2)}) %collective-permute-start.21) | collective-permute-done | bytes 147488 | tf_op jit(solution)/shard_map/ppermute | solution.py:366
  45.5 6.2 %collective-permute-start.23 = (bf16[2,144,256]{2,1,0:T(8,128)(2,1)S(1)}, bf16[2,144,256]{2,1,0:T(8,128)(2,1)S(1)}, u32[]{:S(2)}, u32[]{:S(2)}) collective-permute-start(bf16[2,144,256]{2,1,0:T(8,128)(2,1)S(1)} %maximum_select_fusion.2), channel_id=1, source_target_pairs={{0,2},{2,4},{4,6},{6,0},{1,3},{3,5},{5,7},{7,1},{8,10},{10,12},{12... | collective-permute-start | bytes 442376 | tf_op jit(solution)/shard_map/ppermute | solution.py:366
  51.8 2.7 collective-permute-done.22
  60.8 2.2 collective-permute-start.14
  66.3 1.6 collective-permute-start.18
  71.8 3.6 %all-to-all-start = ((bf16[32,1,128]{2,1,0:T(2,128)(2,1)}), bf16[32,1,128]{2,1,0:T(2,128)(2,1)S(1)}, u32[]{:S(2)}, u32[]{:S(2)}) async-start(bf16[32,1,128]{2,1,0:T(2,128)(2,1)} %broadcast_in_dim.67), calls=%async_computation | async-start | bytes 32768 | tf_op jit(solution)/shard_map/all_to_all | solution.py:442
  75.5 10.1 %all-to-all-done = bf16[32,1,128]{2,1,0:T(2,128)(2,1)S(1)} async-done(((bf16[32,1,128]{2,1,0:T(2,128)(2,1)}), bf16[32,1,128]{2,1,0:T(2,128)(2,1)S(1)}, u32[]{:S(2)}, u32[]{:S(2)}) %all-to-all-start) | async-done | bytes 8224 | tf_op jit(solution)/shard_map/all_to_all | solution.py:442
  89.9 2.1 collective-permute-done.13.refs_12_
  96.3 3.9 %collective-permute-done.24.refs_11_ = bf16[576,256]{1,0:T(8,128)(2,1)S(1)} collective-permute-done((bf16[576,256]{1,0:T(8,128)(2,1)S(1)}, bf16[576,256]{1,0:T(8,128)(2,1)S(1)}, u32[]{:S(2)}, u32[]{:S(2)}) %collective-permute-start.24) | collective-permute-done | bytes 294944 | tf_op jit(solution)/shard_map/ppermute | solution.py:373
  110.5 28.4 %attend.1 = (bf16[8,256,512]{2,1,0:T(8,128)(2,1)S(1)}, bf16[8,64,768]{2,1,0:T(8,128)(2,1)S(1)}, bf16[8,256,256]{2,1,0:T(8,128)(2,1)S(1)}, bf16[8,256,256]{2,1,0:...) custom-call(s32[5]{0:T(128)S(1)} %stack.141.refs_0_, ...), custom_call_target="tpu_custom_call" | custom-call | flops 4831838208 | bytes 8388608 | tf_op jit(solution)/shard_map/attend/pallas_call | solution.py:456
  156.4 17.5 %ffn.1 = (bf16[2,256,512]{2,1,0:T(8,128)(2,1)}, f32[2,256,512]{2,1,0:T(8,128)}, bf16[2,256,256]{2,1,0:T(8,128)(2,1)S(1)}, bf16[2,256,256]{2,1,0:T(8,128)(2,1)}, ...) custom-call(s32[5]{0:T(128)S(1)} %stack.141.refs_0_, ...), custom_call_target="tpu_custom_call" | custom-call | flops 7247757312 | bytes 20971520 | tf_op jit(solution)/shard_map/ffn/pallas_call | solution.py:487
  180.7 32.5 %back.1 = (bf16[4,256,512]{2,1,0:T(8,128)(2,1)}, bf16[4,256,512]{2,1,0:T(8,128)(2,1)}, bf16[512,768]{1,0:T(8,128)(2,1)}, f32[2,256]{1,0:T(2,128)}) custom-call(s32[5]{0:T(128)} %copy-done, bf16[8,256,512]{2,1,0:T(8,128)(2,1)} %copy-done.24, bf16[8,64,768]{2,1,0:T(8,128)(2,1)} %copy-done.28, bf16[8,256,256]{2,1,0:T(8,128)(2,1)} %copy-done.25, ...), custom_call_target="tpu_custom_call" | custom-call | flops 12079595520 | bytes 12582912 | tf_op jit(solution)/shard_map/back/pallas_call | solution.py:546
  215.0 5.3 %all-to-all-start.1 = ((f32[32,1,130]{2,1,0:T(1,128)}), f32[32,1,130]{2,1,0:T(1,128)S(1)}, u32[]{:S(2)}, u32[]{:S(2)}) async-start(f32[32,1,130]{2,1,0:T(1,128)} %all_to_all.11), calls=%async_computation.1 | async-start | bytes 65536 | tf_op jit(solution)/shard_map/all_to_all | solution.py:602
  221.5 1.8 collective-permute-start.45
  225.7 1.8 all-to-all-done.1
  228.9 1.7 collective-permute-start.46
  233.6 1.8 collective-permute-done.48
  236.9 2.3 collective-permute-start.50
  243.5 2.2 add_convert_fusion
  252.8 9.9 %collective-permute-done.54 = bf16[2,576,256]{2,1,0:T(8,128)(2,1)} collective-permute-done((bf16[2,576,256]{2,1,0:T(8,128)(2,1)}, bf16[2,576,256]{2,1,0:T(8,128)(2,1)}, u32[]{:S(2)}, u32[]{:S(2)}) %collective-permute-start.54) | collective-permute-done | bytes 589856 | tf_op jit(solution)/shard_map/ppermute | solution.py:390
  267.8 3.1 %collective-permute-start.43 = (bf16[256,512]{1,0:T(8,128)(2,1)S(1)}, bf16[256,512]{1,0:T(8,128)(2,1)S(1)}, u32[]{:S(2)}, u32[]{:S(2)}) collective-permute-start(bf16[256,512]{1,0:T(8,128)(2,1)S(1)} %get-tuple-element.74), channel_id=1, source_target_pairs={{0,4},{2,6},{4,0},{6,2},{1,5},{3,7},{5,1},{7,3},{8,12},{10,14},{12... | collective-permute-start | bytes 786440 | tf_op jit(solution)/shard_map/ppermute | solution.py:575
  271.0 1.7 collective-permute-done.55
  272.8 2.0 collective-permute-done.57
  275.7 3.2 %collective-permute-start.59 = (bf16[2,144,256]{2,1,0:T(8,128)(2,1)S(1)}, bf16[2,144,256]{2,1,0:T(8,128)(2,1)S(1)}, u32[]{:S(2)}, u32[]{:S(2)}) collective-permute-start(bf16[2,144,256]{2,1,0:T(8,128)(2,1)S(1)} %get-tuple-element.79), channel_id=1, source_target_pairs={{0,4},{2,6},{4,0},{6,2},{1,5},{3,7},{5,1},{7,3},{8,12},{10,14},{12... | collective-permute-start | bytes 442376 | tf_op jit(solution)/shard_map/ppermute | solution.py:406
  279.0 10.5 %collective-permute-done.43 = bf16[256,512]{1,0:T(8,128)(2,1)S(1)} collective-permute-done((bf16[256,512]{1,0:T(8,128)(2,1)S(1)}, bf16[256,512]{1,0:T(8,128)(2,1)S(1)}, u32[]{:S(2)}, u32[]{:S(2)}) %collective-permute-start.43) | collective-permute-done | bytes 262176 | tf_op jit(solution)/shard_map/ppermute | solution.py:575
  290.8 1.9 collective-permute-done.58
  292.7 10.1 %collective-permute-done.59 = bf16[2,144,256]{2,1,0:T(8,128)(2,1)S(1)} collective-permute-done((bf16[2,144,256]{2,1,0:T(8,128)(2,1)S(1)}, bf16[2,144,256]{2,1,0:T(8,128)(2,1)S(1)}, u32[]{:S(2)}, u32[]{:S(2)}) %collective-permute-start.59) | collective-permute-done | bytes 147488 | tf_op jit(solution)/shard_map/ppermute | solution.py:406
  (330 shorter events, 100.6 us)
Async XLA Ops:
  3.6 31.0 %collective-permute-start.20 = (bf16[144,256]{1,0:T(8,128)(2,1)S(1)}, bf16[144,256]{1,0:T(8,128)(2,1)S(1)}, u32[]{:S(2)}, u32[]{:S(2)}) collective-permute-start(bf16[144,256]{1,0:T(8,128)(2,1)S(1)} %pad_maximum_fusion.4), channel_id=1, source_target_pairs={{0,1},{1,0},{2,3},{3,2},{4,5},{5,4},{6,7},{7,6},{8,9},{9,8},{10,11... | collective-permute-start | bytes 221192 | tf_op jit(solution)/shard_map/ppermute | solution.py:430
  5.5 62.4 %collective-permute-start = (bf16[256,512]{1,0:T(8,128)(2,1)S(1)}, bf16[256,512]{1,0:T(8,128)(2,1)S(1)}, u32[]{:S(2)}, u32[]{:S(2)}) collective-permute-start(bf16[256,512]{1,0:T(8,128)(2,1)S(1)} %get-tuple-element.85), channel_id=1, source_target_pairs={{0,2},{2,4},{4,6},{6,0},{1,3},{3,5},{5,7},{7,1},{8,10},{10,12},{12... | collective-permute-start | bytes 786440 | tf_op jit(solution)/shard_map/ppermute | solution.py:420
  8.4 60.0 %collective-permute-start.1 = (bf16[256,512]{1,0:T(8,128)(2,1)}, bf16[256,512]{1,0:T(8,128)(2,1)S(1)}, u32[]{:S(2)}, u32[]{:S(2)}) collective-permute-start(bf16[256,512]{1,0:T(8,128)(2,1)} %get-tuple-element.87), channel_id=1, source_target_pairs={{0,4},{2,6},{4,0},{6,2},{1,5},{3,7},{5,1},{7,3},{8,12},{10,14},{12... | collective-permute-start | bytes 786440 | tf_op jit(solution)/shard_map/ppermute | solution.py:420
  11.0 58.5 %collective-permute-start.2 = (bf16[256,512]{1,0:T(8,128)(2,1)S(1)}, bf16[256,512]{1,0:T(8,128)(2,1)}, u32[]{:S(2)}, u32[]{:S(2)}) collective-permute-start(bf16[256,512]{1,0:T(8,128)(2,1)S(1)} %get-tuple-element.84), channel_id=1, source_target_pairs={{0,6},{2,0},{4,2},{6,4},{1,7},{3,1},{5,3},{7,5},{8,14},{10,8},{12,... | collective-permute-start | bytes 786440 | tf_op jit(solution)/shard_map/ppermute | solution.py:420
  13.4 16.0 %collective-permute-start.8 = (bf16[32,768]{1,0:T(8,128)(2,1)S(1)}, bf16[32,768]{1,0:T(8,128)(2,1)S(1)}, u32[]{:S(2)}, u32[]{:S(2)}) collective-permute-start(bf16[32,768]{1,0:T(8,128)(2,1)S(1)} %bitcast.248), channel_id=1, source_target_pairs={{0,6},{2,0},{4,2},{6,4},{1,7},{3,1},{5,3},{7,5},{8,14},{10,8},{12,... | collective-permute-start | bytes 147464 | tf_op jit(solution)/shard_map/ppermute | solution.py:366
  36.7 8.8 %collective-permute-start.21 = (bf16[2,144,256]{2,1,0:T(8,128)(2,1)S(1)}, bf16[2,144,256]{2,1,0:T(8,128)(2,1)S(1)}, u32[]{:S(2)}, u32[]{:S(2)}) collective-permute-start(bf16[2,144,256]{2,1,0:T(8,128)(2,1)S(1)} %maximum_select_fusion.2), channel_id=1, source_target_pairs={{0,6},{2,0},{4,2},{6,4},{1,7},{3,1},{5,3},{7,5},{8,14},{10,8},{12,... | collective-permute-start | bytes 442376 | tf_op jit(solution)/shard_map/ppermute | solution.py:366
  41.2 13.2 %collective-permute-start.22 = (bf16[2,144,256]{2,1,0:T(8,128)(2,1)S(1)}, bf16[2,144,256]{2,1,0:T(8,128)(2,1)S(1)}, u32[]{:S(2)}, u32[]{:S(2)}) collective-permute-start(bf16[2,144,256]{2,1,0:T(8,128)(2,1)S(1)} %maximum_select_fusion.2), channel_id=1, source_target_pairs={{0,4},{2,6},{4,0},{6,2},{1,5},{3,7},{5,1},{7,3},{8,12},{10,14},{12... | collective-permute-start | bytes 442376 | tf_op jit(solution)/shard_map/ppermute | solution.py:366
  45.5 10.4 %collective-permute-start.23 = (bf16[2,144,256]{2,1,0:T(8,128)(2,1)S(1)}, bf16[2,144,256]{2,1,0:T(8,128)(2,1)S(1)}, u32[]{:S(2)}, u32[]{:S(2)}) collective-permute-start(bf16[2,144,256]{2,1,0:T(8,128)(2,1)S(1)} %maximum_select_fusion.2), channel_id=1, source_target_pairs={{0,2},{2,4},{4,6},{6,0},{1,3},{3,5},{5,7},{7,1},{8,10},{10,12},{12... | collective-permute-start | bytes 442376 | tf_op jit(solution)/shard_map/ppermute | solution.py:366
  64.5 22.1 %collective-permute-start.3 = (bf16[256,512]{1,0:T(8,128)(2,1)S(1)}, bf16[256,512]{1,0:T(8,128)(2,1)S(1)}, u32[]{:S(2)}, u32[]{:S(2)}) collective-permute-start(bf16[256,512]{1,0:T(8,128)(2,1)S(1)} %get-tuple-element.86.refs_1_), channel_id=1, source_target_pairs={{0,1},{1,0},{2,3},{3,2},{4,5},{5,4},{6,7},{7,6},{8,9},{9,8},{10,11... | collective-permute-start | bytes 786440 | tf_op jit(solution)/shard_map/ppermute | solution.py:422
  66.3 21.6 %collective-permute-start.18 = (bf16[256,512]{1,0:T(8,128)(2,1)}, bf16[256,512]{1,0:T(8,128)(2,1)S(1)}, u32[]{:S(2)}, u32[]{:S(2)}) collective-permute-start(bf16[256,512]{1,0:T(8,128)(2,1)} %get-tuple-element.83), channel_id=1, source_target_pairs={{0,0},{4,4},{3,1},{7,5},{2,2},{6,6},{1,3},{5,7},{8,8},{12,12},{11,... | collective-permute-start | bytes 786440 | tf_op jit(solution)/shard_map/ppermute | solution.py:451
  67.9 21.3 %collective-permute-start.19 = (bf16[256,512]{1,0:T(8,128)(2,1)}, bf16[256,512]{1,0:T(8,128)(2,1)S(1)}, u32[]{:S(2)}, u32[]{:S(2)}) collective-permute-start(bf16[256,512]{1,0:T(8,128)(2,1)} %get-tuple-element.82), channel_id=1, source_target_pairs={{4,0},{0,4},{7,1},{3,5},{6,2},{2,6},{5,3},{1,7},{12,8},{8,12},{15,... | collective-permute-start | bytes 786440 | tf_op jit(solution)/shard_map/ppermute | solution.py:452
  68.5 24.7 %collective-permute-start.28 = (bf16[576,256]{1,0:T(8,128)(2,1)S(1)}, bf16[576,256]{1,0:T(8,128)(2,1)S(1)}, u32[]{:S(2)}, u32[]{:S(2)}) collective-permute-start(bf16[576,256]{1,0:T(8,128)(2,1)S(1)} %slice.163.refs_14_), channel_id=1, source_target_pairs={{0,16},{16,0},{1,17},{17,1},{2,18},{18,2},{3,19},{19,3},{4,20},{20... | collective-permute-start | bytes 884744 | tf_op jit(solution)/shard_map/ppermute | solution.py:374
  69.6 24.1 %collective-permute-start.27 = (bf16[576,256]{1,0:T(8,128)(2,1)S(1)}, bf16[576,256]{1,0:T(8,128)(2,1)S(1)}, u32[]{:S(2)}, u32[]{:S(2)}) collective-permute-start(bf16[576,256]{1,0:T(8,128)(2,1)S(1)} %slice.163.refs_14_), channel_id=1, source_target_pairs={{0,8},{8,0},{1,9},{9,1},{2,10},{10,2},{3,11},{11,3},{4,12},{12,4},... | collective-permute-start | bytes 884744 | tf_op jit(solution)/shard_map/ppermute | solution.py:381
  71.8 13.8 %all-to-all-start = ((bf16[32,1,128]{2,1,0:T(2,128)(2,1)}), bf16[32,1,128]{2,1,0:T(2,128)(2,1)S(1)}, u32[]{:S(2)}, u32[]{:S(2)}) async-start(bf16[32,1,128]{2,1,0:T(2,128)(2,1)} %broadcast_in_dim.67), calls=%async_computation | async-start | bytes 32768 | tf_op jit(solution)/shard_map/all_to_all | solution.py:442
  94.7 52.5 %collective-permute-start.25 = (bf16[576,256]{1,0:T(8,128)(2,1)S(1)}, bf16[576,256]{1,0:T(8,128)(2,1)S(1)}, u32[]{:S(2)}, u32[]{:S(2)}) collective-permute-start(bf16[576,256]{1,0:T(8,128)(2,1)S(1)} %pad_maximum_fusion.1.refs_10_), channel_id=1, source_target_pairs={{0,16},{16,0},{1,17},{17,1},{2,18},{18,2},{3,19},{19,3},{4,20},{20... | collective-permute-start | bytes 884744 | tf_op jit(solution)/shard_map/ppermute | solution.py:378
  100.2 47.0 %collective-permute-start.30 = (bf16[576,256]{1,0:T(8,128)(2,1)S(1)}, bf16[576,256]{1,0:T(8,128)(2,1)S(1)}, u32[]{:S(2)}, u32[]{:S(2)}) collective-permute-start(bf16[576,256]{1,0:T(8,128)(2,1)S(1)} %pad_maximum_fusion.1.refs_10_), channel_id=1, source_target_pairs={{0,1},{1,0},{2,3},{3,2},{4,5},{5,4},{6,7},{7,6},{8,9},{9,8},{10,11... | collective-permute-start | bytes 884744 | tf_op jit(solution)/shard_map/ppermute | solution.py:439
  100.2 49.3 %collective-permute-start.29 = (bf16[576,256]{1,0:T(8,128)(2,1)S(1)}, bf16[576,256]{1,0:T(8,128)(2,1)S(1)}, u32[]{:S(2)}, u32[]{:S(2)}) collective-permute-start(bf16[576,256]{1,0:T(8,128)(2,1)S(1)} %collective-permute-done.28.refs_16_), channel_id=1, source_target_pairs={{0,8},{8,0},{1,9},{9,1},{2,10},{10,2},{3,11},{11,3},{4,12},{12,4},... | collective-permute-start | bytes 884744 | tf_op jit(solution)/shard_map/ppermute | solution.py:381
  101.5 48.4 %collective-permute-start.35 = (bf16[576,256]{1,0:T(8,128)(2,1)S(1)}, bf16[576,256]{1,0:T(8,128)(2,1)S(1)}, u32[]{:S(2)}, u32[]{:S(2)}) collective-permute-start(bf16[576,256]{1,0:T(8,128)(2,1)S(1)} %collective-permute-done.27.refs_15_), channel_id=1, source_target_pairs={{0,1},{1,0},{2,3},{3,2},{4,5},{5,4},{6,7},{7,6},{8,9},{9,8},{10,11... | collective-permute-start | bytes 884744 | tf_op jit(solution)/shard_map/ppermute | solution.py:439
  101.7 48.4 %collective-permute-start.26 = (bf16[576,256]{1,0:T(8,128)(2,1)S(1)}, bf16[576,256]{1,0:T(8,128)(2,1)}, u32[]{:S(2)}, u32[]{:S(2)}) collective-permute-start(bf16[576,256]{1,0:T(8,128)(2,1)S(1)} %collective-permute-done.24.refs_11_), channel_id=1, source_target_pairs={{0,16},{16,0},{1,17},{17,1},{2,18},{18,2},{3,19},{19,3},{4,20},{20... | collective-permute-start | bytes 884744 | tf_op jit(solution)/shard_map/ppermute | solution.py:378
  174.9 68.5 %collective-permute-start.53 = (bf16[4,1152,256]{2,1,0:T(8,128)(2,1)}, bf16[4,1152,256]{2,1,0:T(8,128)(2,1)}, u32[]{:S(2)}, u32[]{:S(2)}) collective-permute-start(bf16[4,1152,256]{2,1,0:T(8,128)(2,1)} %get-tuple-element.58), channel_id=1, source_target_pairs={{0,1},{1,0},{2,3},{3,2},{4,5},{5,4},{6,7},{7,6},{8,9},{9,8},{10,11... | collective-permute-start | bytes 7077896 | tf_op jit(solution)/shard_map/ppermute | solution.py:527
  179.1 45.8 %collective-permute-start.38 = (bf16[256,512]{1,0:T(8,128)(2,1)S(1)}, bf16[256,512]{1,0:T(8,128)(2,1)S(1)}, u32[]{:S(2)}, u32[]{:S(2)}) collective-permute-start(bf16[256,512]{1,0:T(8,128)(2,1)S(1)} %get-tuple-element.80), channel_id=1, source_target_pairs={{0,0},{4,4},{1,3},{5,7},{2,2},{6,6},{3,1},{7,5},{8,8},{12,12},{9,1... | collective-permute-start | bytes 786440 | tf_op jit(solution)/shard_map/ppermute | solution.py:523
  179.8 45.1 %collective-permute-start.39 = (bf16[256,512]{1,0:T(8,128)(2,1)S(1)}, bf16[256,512]{1,0:T(8,128)(2,1)S(1)}, u32[]{:S(2)}, u32[]{:S(2)}) collective-permute-start(bf16[256,512]{1,0:T(8,128)(2,1)S(1)} %get-tuple-element.81), channel_id=1, source_target_pairs={{0,4},{4,0},{1,7},{5,3},{2,6},{6,2},{3,5},{7,1},{8,12},{12,8},{9,1... | collective-permute-start | bytes 786440 | tf_op jit(solution)/shard_map/ppermute | solution.py:524
  215.0 12.5 %all-to-all-start.1 = ((f32[32,1,130]{2,1,0:T(1,128)}), f32[32,1,130]{2,1,0:T(1,128)S(1)}, u32[]{:S(2)}, u32[]{:S(2)}) async-start(f32[32,1,130]{2,1,0:T(1,128)} %all_to_all.11), calls=%async_computation.1 | async-start | bytes 65536 | tf_op jit(solution)/shard_map/all_to_all | solution.py:602
  224.9 26.5 %collective-permute-start.41 = (bf16[4,256,512]{2,1,0:T(8,128)(2,1)}, bf16[4,256,512]{2,1,0:T(8,128)(2,1)}, u32[]{:S(2)}, u32[]{:S(2)}) collective-permute-start(bf16[4,256,512]{2,1,0:T(8,128)(2,1)} %get-tuple-element.50), channel_id=1, source_target_pairs={{0,1},{1,0},{2,3},{3,2},{4,5},{5,4},{6,7},{7,6},{8,9},{9,8},{10,11... | collective-permute-start | bytes 3145736 | tf_op jit(solution)/shard_map/ppermute | solution.py:573
  246.7 16.0 %collective-permute-start.54 = (bf16[2,576,256]{2,1,0:T(8,128)(2,1)}, bf16[2,576,256]{2,1,0:T(8,128)(2,1)}, u32[]{:S(2)}, u32[]{:S(2)}) collective-permute-start(bf16[2,576,256]{2,1,0:T(8,128)(2,1)} %dynamic-slice_bitcast_fusion.1), channel_id=1, source_target_pairs={{0,8},{8,0},{1,9},{9,1},{2,10},{10,2},{3,11},{11,3},{4,12},{12,4},... | collective-permute-start | bytes 1769480 | tf_op jit(solution)/shard_map/ppermute | solution.py:390
  250.7 15.5 %collective-permute-start.56 = (bf16[2,576,256]{2,1,0:T(8,128)(2,1)S(1)}, bf16[2,576,256]{2,1,0:T(8,128)(2,1)S(1)}, u32[]{:S(2)}, u32[]{:S(2)}) collective-permute-start(bf16[2,576,256]{2,1,0:T(8,128)(2,1)S(1)} %dynamic-slice_bitcast_fusion), channel_id=1, source_target_pairs={{0,16},{16,0},{1,17},{17,1},{2,18},{18,2},{3,19},{19,3},{4,20},{20... | collective-permute-start | bytes 1769480 | tf_op jit(solution)/shard_map/ppermute | solution.py:390
  267.1 11.8 %collective-permute-start.42 = (bf16[256,512]{1,0:T(8,128)(2,1)S(1)}, bf16[256,512]{1,0:T(8,128)(2,1)S(1)}, u32[]{:S(2)}, u32[]{:S(2)}) collective-permute-start(bf16[256,512]{1,0:T(8,128)(2,1)S(1)} %get-tuple-element.72), channel_id=1, source_target_pairs={{0,2},{2,4},{4,6},{6,0},{1,3},{3,5},{5,7},{7,1},{8,10},{10,12},{12... | collective-permute-start | bytes 786440 | tf_op jit(solution)/shard_map/ppermute | solution.py:575
  267.8 21.7 %collective-permute-start.43 = (bf16[256,512]{1,0:T(8,128)(2,1)S(1)}, bf16[256,512]{1,0:T(8,128)(2,1)S(1)}, u32[]{:S(2)}, u32[]{:S(2)}) collective-permute-start(bf16[256,512]{1,0:T(8,128)(2,1)S(1)} %get-tuple-element.74), channel_id=1, source_target_pairs={{0,4},{2,6},{4,0},{6,2},{1,5},{3,7},{5,1},{7,3},{8,12},{10,14},{12... | collective-permute-start | bytes 786440 | tf_op jit(solution)/shard_map/ppermute | solution.py:575
  270.9 18.6 %collective-permute-start.44 = (bf16[256,512]{1,0:T(8,128)(2,1)S(1)}, bf16[256,512]{1,0:T(8,128)(2,1)S(1)}, u32[]{:S(2)}, u32[]{:S(2)}) collective-permute-start(bf16[256,512]{1,0:T(8,128)(2,1)S(1)} %get-tuple-element.73), channel_id=1, source_target_pairs={{0,6},{2,0},{4,2},{6,4},{1,7},{3,1},{5,3},{7,5},{8,14},{10,8},{12,... | collective-permute-start | bytes 786440 | tf_op jit(solution)/shard_map/ppermute | solution.py:575
  275.0 17.6 %collective-permute-start.58 = (bf16[2,144,256]{2,1,0:T(8,128)(2,1)S(1)}, bf16[2,144,256]{2,1,0:T(8,128)(2,1)S(1)}, u32[]{:S(2)}, u32[]{:S(2)}) collective-permute-start(bf16[2,144,256]{2,1,0:T(8,128)(2,1)S(1)} %get-tuple-element.77), channel_id=1, source_target_pairs={{0,2},{2,4},{4,6},{6,0},{1,3},{3,5},{5,7},{7,1},{8,10},{10,12},{12... | collective-permute-start | bytes 442376 | tf_op jit(solution)/shard_map/ppermute | solution.py:406
  275.7 27.1 %collective-permute-start.59 = (bf16[2,144,256]{2,1,0:T(8,128)(2,1)S(1)}, bf16[2,144,256]{2,1,0:T(8,128)(2,1)S(1)}, u32[]{:S(2)}, u32[]{:S(2)}) collective-permute-start(bf16[2,144,256]{2,1,0:T(8,128)(2,1)S(1)} %get-tuple-element.79), channel_id=1, source_target_pairs={{0,4},{2,6},{4,0},{6,2},{1,5},{3,7},{5,1},{7,3},{8,12},{10,14},{12... | collective-permute-start | bytes 442376 | tf_op jit(solution)/shard_map/ppermute | solution.py:406
  278.9 23.9 %collective-permute-start.60 = (bf16[2,144,256]{2,1,0:T(8,128)(2,1)S(1)}, bf16[2,144,256]{2,1,0:T(8,128)(2,1)S(1)}, u32[]{:S(2)}, u32[]{:S(2)}) collective-permute-start(bf16[2,144,256]{2,1,0:T(8,128)(2,1)S(1)} %get-tuple-element.78), channel_id=1, source_target_pairs={{0,6},{2,0},{4,2},{6,4},{1,7},{3,1},{5,3},{7,5},{8,14},{10,8},{12,... | collective-permute-start | bytes 442376 | tf_op jit(solution)/shard_map/ppermute | solution.py:406
  (78 other events, 510.5 us)
